TPU v7x, 256 devices: a whole 4x4x8 slice. The times are simulated.
256 devices in a mesh: gx: 4 (over y_lo, core), gy: 4 (over x), gz: 16 (over y_hi, z).
Axes of the slice: x: 4, y: 4 (y_hi: 2, y_lo: 2; y = y_hi * 2 + y_lo), z: 8, core: 2. Of those that a mesh axis runs over, the one named last changes fastest.
Arguments:
- field: float32 [512, 1024, 1024], P('gz', 'gy', 'gx'), may hold values from -6 to 6
Outputs:
- picture: float32 [4, 1024, 1024], P(None, ('gy', 'gz'), 'gx')
All inputs are finite; a program needn't handle non-finite values.
Results may differ from a plain program's by a relative error of at most 0.00002.
Values sent between devices are 32-bit elements; how exact they have to be, the bound alone decides.
No kernel may reach another device: no remote copies, remote signals or barrier semaphores. Data moves between devices by JAX's collectives and lax.ppermute only.
A program may use at most 128 MiB of HBM per device.

v0:
```python
import jax
import jax.numpy as jnp
from jax import lax
from jax.sharding import PartitionSpec as P


def padded_2(block, sides, width):
    for axis, dim in sides:
        count = lax.axis_size(axis)
        forward = [(i, i + 1) for i in range(count - 1)]
        backward = [(target, source) for source, target in forward]
        low = lax.ppermute(
            lax.slice_in_dim(block, block.shape[dim] - width, None, axis=dim), axis, forward
        )
        high = lax.ppermute(lax.slice_in_dim(block, 0, width, axis=dim), axis, backward)
        block = jnp.concatenate([low, block, high], axis=dim)
    return block


def sample_light(centre_slice, grad_x, grad_y, grad_z, density):
    squared = grad_x * grad_x + grad_y * grad_y + grad_z * grad_z
    shading = 0.25 + 0.75 * jnp.abs((grad_x + 2.0 * grad_y + 2.0 * grad_z) / 3.0) / jnp.sqrt(
        squared + 1.0
    )
    extinction = density * (1.0 + jnp.tanh(centre_slice)) * (0.2 + squared / (1.0 + squared))
    opacity = 1.0 - jnp.exp(-extinction)
    emitted = jnp.stack(
        [
            jax.nn.sigmoid(2.0 * centre_slice) * shading,
            jnp.exp(-centre_slice * centre_slice) * shading,
            jax.nn.sigmoid(-2.0 * centre_slice) * shading,
        ]
    )
    return (opacity, emitted)


def composite_over(nearer, farther):
    return nearer + (1.0 - nearer[3:4]) * farther


def per_device(field):
    depth_cells, row_cells, column_cells = field.shape
    depth_groups = lax.axis_size("gz")
    bit_count = depth_groups.bit_length() - 1
    density = 4.0 / (depth_cells * depth_groups)
    padded = padded_2(field, (("gx", 2), ("gy", 1), ("gz", 0)), 1)

    def march(state_pair, block_number):
        colour_sum, transmit = state_pair
        slab_block = lax.dynamic_slice_in_dim(padded, block_number * 4, 6, 0)
        centre_slice = slab_block[1:5, 1:-1, 1:-1]
        grad_x = (slab_block[1:5, 1:-1, 2:] - slab_block[1:5, 1:-1, :-2]) * 0.5
        grad_y = (slab_block[1:5, 2:, 1:-1] - slab_block[1:5, :-2, 1:-1]) * 0.5
        grad_z = (slab_block[2:6, 1:-1, 1:-1] - slab_block[0:4, 1:-1, 1:-1]) * 0.5
        opacity, emitted = sample_light(centre_slice, grad_x, grad_y, grad_z, density)
        through = jnp.cumprod(1.0 - opacity, axis=0)
        before = jnp.concatenate([jnp.ones_like(through[:1]), through[:-1]], axis=0)
        weights = transmit[None] * before * opacity
        colour_sum = colour_sum + jnp.sum(weights[None] * emitted, axis=1)
        transmit = transmit * through[-1]
        return ((colour_sum, transmit), None)

    start = (
        jnp.zeros((3, row_cells, column_cells), jnp.float32),
        jnp.ones((row_cells, column_cells), jnp.float32),
    )
    (colour_sum, transmit), unused = lax.scan(
        march, start, jnp.arange(depth_cells // 4, dtype=jnp.int32)
    )
    partial_image = jnp.concatenate([colour_sum, (1.0 - transmit)[None]], axis=0)
    band_rows = row_cells // depth_groups
    tiled = partial_image.reshape(4, depth_groups, band_rows, column_cells)
    stacked = lax.all_to_all(tiled, "gz", split_axis=1, concat_axis=1, tiled=True)
    for level in range(bit_count):
        stacked = composite_over(stacked[:, 0::2], stacked[:, 1::2])
    return stacked[:, 0]


def solution(mesh):
    return jax.shard_map(
        per_device,
        mesh=mesh,
        in_specs=(P("gz", "gy", "gx"),),
        out_specs=P(None, ("gy", "gz"), "gx"),
        check_vma=False,
    )
```

profile of v0, /device:TPU:32, one launch (start us, length us, event | category | flops | bytes accessed | tf_op | source)
XLA Modules:
  0.0 301.4 jit_solution(2073560132430454827)
XLA Ops:
  0.0 7.9 %fusion.24 = (f32[32,256,1]{2,1,0:T(8,128)}, f32[32,256,1]{2,1,0:T(8,128)}) fusion(f32[32,256,256]{2,1,0:T(8,128)} %param.3), kind=kLoop, calls=%fused_computation.56 | loop fusion | bytes 131072 | tf_op jit(solution)/shard_map/slice | solution.py:13
  7.9 2.8 copy.7
  10.7 1.7 collective-permute-start
  12.5 2.8 copy.8
  15.3 1.3 collective-permute-start.1
  16.6 2.7 copy.4
  19.8 2.6 copy.5
  22.4 1.7 pad_maximum_fusion.9
  24.2 3.7 %collective-permute-start.2 = (f32[32,1,258]{2,1,0:T(1,128)S(1)}, f32[32,1,258]{2,1,0:T(1,128)S(1)}, u32[]{:S(2)}, u32[]{:S(2)}) collective-permute-start(f32[32,1,258]{2,1,0:T(1,128)S(1)} %get-tuple-element.126), channel_id=1, source_target_pairs={{0,16},{16,32},{32,48},{1,17},{17,33},{33,49},{2,18},{18,34},{34,5... | collective-permute-start | bytes 99080 | tf_op jit(solution)/shard_map/ppermute | solution.py:12
  27.8 1.3 collective-permute-start.3
  29.6 4.3 %collective-permute-done.3 = f32[32,1,258]{2,1,0:T(1,128)S(1)} collective-permute-done((f32[32,1,258]{2,1,0:T(1,128)S(1)}, f32[32,1,258]{2,1,0:T(1,128)S(1)}, u32[]{:S(2)}, u32[]{:S(2)}) %collective-permute-start.3) | collective-permute-done | bytes 33056 | tf_op jit(solution)/shard_map/ppermute | solution.py:15
  33.8 1.4 pad_maximum_fusion.6
  35.2 3.8 %collective-permute-start.4 = (f32[1,258,258]{2,1,0:T(8,128)S(1)}, f32[1,258,258]{2,1,0:T(8,128)S(1)}, u32[]{:S(2)}, u32[]{:S(2)}) collective-permute-start(f32[1,258,258]{2,1,0:T(8,128)S(1)} %get-tuple-element.124), channel_id=1, source_target_pairs={{0,1},{1,2},{2,3},{3,4},{4,5},{5,6},{6,7},{7,8},{8,9},{9,10},{10,1... | collective-permute-start | bytes 798776 | tf_op jit(solution)/shard_map/ppermute | solution.py:12
  39.0 2.2 collective-permute-start.5
  41.3 7.8 %collective-permute-done.4 = f32[1,258,258]{2,1,0:T(8,128)S(1)} collective-permute-done((f32[1,258,258]{2,1,0:T(8,128)S(1)}, f32[1,258,258]{2,1,0:T(8,128)S(1)}, u32[]{:S(2)}, u32[]{:S(2)}) %collective-permute-start.4) | collective-permute-done | bytes 266288 | tf_op jit(solution)/shard_map/ppermute | solution.py:12
  49.1 3.9 %collective-permute-done.5 = f32[1,258,258]{2,1,0:T(8,128)S(1)} collective-permute-done((f32[1,258,258]{2,1,0:T(8,128)S(1)}, f32[1,258,258]{2,1,0:T(8,128)S(1)}, u32[]{:S(2)}, u32[]{:S(2)}) %collective-permute-start.5) | collective-permute-done | bytes 266288 | tf_op jit(solution)/shard_map/ppermute | solution.py:15
  53.1 19.6 %pad_maximum_fusion = f32[34,258,258]{2,1,0:T(8,128)} fusion(f32[1,258,258]{2,1,0:T(8,128)S(1)} %collective-permute-done.5, f32[32,1,258]{2,1,0:T(1,128)S(1)} %collective-permute-done.3, f32[32,256,1]{2,1,0:T(8,128)} %copy.5, f32[32,256,256]{2,1,0:T(8,128)} %param.3, f32[32,256,1]{2,1,0:T(8,128)} %copy.4, f32[32,1,258]{2,1,0:T(1,128)S(1)} %collective-permute-done.2, ...), kind=kLoop, calls=%fused_computation.31 | loop fusion | flops 13579056 | bytes 18105408 | tf_op jit(solution)/shard_map/concatenate | solution.py:16
  72.7 188.1 %while.16 = (s32[]{:T(128)}, f32[3,256,256]{2,1,0:T(8,128)}, f32[256,256]{1,0:T(8,128)S(1)}, s32[8]{0:T(128)S(1)}, f32[34,258,258]{2,1,0:T(8,128)}, /*index=5*/s...) while((s32[]{:T(128)}, f32[3,256,256]{2,1,0:T(8,128)}, ...), condition=%wide.region_3.4_spmd.clone, body=%wide.region_0.3_spmd.clone.sunk | while | flops 18415628 | bytes 46661980 | solution.py:67
  74.0 7.8 %multiply_bitcast_fusion.3 = (f32[1,4,256,256]{3,2,1,0:T(8,128)}, f32[4,256,256]{2,1,0:T(8,128)S(1)}) fusion(f32[34,258,258]{2,1,0:T(8,128)} %get-tuple-element.201, s32[]{:T(128)S(6)} %add.207, s32[]{:T(128)S(6)} %add.208, s32[]{:T(128)S(6)} %select_n.9, s32[]{:T(128)S(6)} %add.209, s32[]{:T(128)S(6)} %add.210), kind=kLoop, calls=%fused_computation.20.clone.1 | loop fusion | flops 6291456 | bytes 9437204 | tf_op jit(solution)/shard_map/while/body/eval_jaxpr/stack | solution.py:27
  81.8 7.0 %fusion.31 = (f32[1,4,256,256]{3,2,1,0:T(8,128)S(1)}, f32[1,4,256,256]{3,2,1,0:T(8,128)S(1)}, f32[4,256,256]{2,1,0:T(8,128)S(1)}) fusion(f32[4,256,256]{2,1,0:T(8,128)S(1)} %get-tuple-element.168, f32[34,258,258]{2,1,0:T(8,128)} %get-tuple-element.201, s32[]{:T(128)S(6)} %add.207, s32[]{:T(128)S(6)} %add.208, s32[]{:T(128)S(6)} %select_n.9, ...), kind=kLoop, calls=%fused_computation.14.clone.1 | loop fusion | flops 7077888 | bytes 11534356 | tf_op jit(solution)/shard_map/while/body/eval_jaxpr/stack | solution.py:27
  89.0 1.0 copy-done
  90.9 1.1 fusion.33
  92.0 1.3 multiply_multiply_fusion.2
  93.3 1.6 fusion.34
  97.5 7.8 %multiply_bitcast_fusion.3 = (f32[1,4,256,256]{3,2,1,0:T(8,128)}, f32[4,256,256]{2,1,0:T(8,128)S(1)}) fusion(f32[34,258,258]{2,1,0:T(8,128)} %get-tuple-element.201, s32[]{:T(128)S(6)} %add.207, s32[]{:T(128)S(6)} %add.208, s32[]{:T(128)S(6)} %select_n.9, s32[]{:T(128)S(6)} %add.209, s32[]{:T(128)S(6)} %add.210), kind=kLoop, calls=%fused_computation.20.clone.1 | loop fusion | flops 6291456 | bytes 9437204 | tf_op jit(solution)/shard_map/while/body/eval_jaxpr/stack | solution.py:27
  105.3 7.0 %fusion.31 = (f32[1,4,256,256]{3,2,1,0:T(8,128)S(1)}, f32[1,4,256,256]{3,2,1,0:T(8,128)S(1)}, f32[4,256,256]{2,1,0:T(8,128)S(1)}) fusion(f32[4,256,256]{2,1,0:T(8,128)S(1)} %get-tuple-element.168, f32[34,258,258]{2,1,0:T(8,128)} %get-tuple-element.201, s32[]{:T(128)S(6)} %add.207, s32[]{:T(128)S(6)} %add.208, s32[]{:T(128)S(6)} %select_n.9, ...), kind=kLoop, calls=%fused_computation.14.clone.1 | loop fusion | flops 7077888 | bytes 11534356 | tf_op jit(solution)/shard_map/while/body/eval_jaxpr/stack | solution.py:27
  112.4 1.0 copy-done
  114.4 1.1 fusion.33
  115.5 1.3 multiply_multiply_fusion.2
  116.7 1.6 fusion.34
  120.9 7.8 %multiply_bitcast_fusion.3 = (f32[1,4,256,256]{3,2,1,0:T(8,128)}, f32[4,256,256]{2,1,0:T(8,128)S(1)}) fusion(f32[34,258,258]{2,1,0:T(8,128)} %get-tuple-element.201, s32[]{:T(128)S(6)} %add.207, s32[]{:T(128)S(6)} %add.208, s32[]{:T(128)S(6)} %select_n.9, s32[]{:T(128)S(6)} %add.209, s32[]{:T(128)S(6)} %add.210), kind=kLoop, calls=%fused_computation.20.clone.1 | loop fusion | flops 6291456 | bytes 9437204 | tf_op jit(solution)/shard_map/while/body/eval_jaxpr/stack | solution.py:27
  128.6 7.0 %fusion.31 = (f32[1,4,256,256]{3,2,1,0:T(8,128)S(1)}, f32[1,4,256,256]{3,2,1,0:T(8,128)S(1)}, f32[4,256,256]{2,1,0:T(8,128)S(1)}) fusion(f32[4,256,256]{2,1,0:T(8,128)S(1)} %get-tuple-element.168, f32[34,258,258]{2,1,0:T(8,128)} %get-tuple-element.201, s32[]{:T(128)S(6)} %add.207, s32[]{:T(128)S(6)} %add.208, s32[]{:T(128)S(6)} %select_n.9, ...), kind=kLoop, calls=%fused_computation.14.clone.1 | loop fusion | flops 7077888 | bytes 11534356 | tf_op jit(solution)/shard_map/while/body/eval_jaxpr/stack | solution.py:27
  135.8 1.0 copy-done
  137.7 1.1 fusion.33
  138.8 1.3 multiply_multiply_fusion.2
  140.1 1.6 fusion.34
  144.2 7.9 %multiply_bitcast_fusion.3 = (f32[1,4,256,256]{3,2,1,0:T(8,128)}, f32[4,256,256]{2,1,0:T(8,128)S(1)}) fusion(f32[34,258,258]{2,1,0:T(8,128)} %get-tuple-element.201, s32[]{:T(128)S(6)} %add.207, s32[]{:T(128)S(6)} %add.208, s32[]{:T(128)S(6)} %select_n.9, s32[]{:T(128)S(6)} %add.209, s32[]{:T(128)S(6)} %add.210), kind=kLoop, calls=%fused_computation.20.clone.1 | loop fusion | flops 6291456 | bytes 9437204 | tf_op jit(solution)/shard_map/while/body/eval_jaxpr/stack | solution.py:27
  152.1 7.1 %fusion.31 = (f32[1,4,256,256]{3,2,1,0:T(8,128)S(1)}, f32[1,4,256,256]{3,2,1,0:T(8,128)S(1)}, f32[4,256,256]{2,1,0:T(8,128)S(1)}) fusion(f32[4,256,256]{2,1,0:T(8,128)S(1)} %get-tuple-element.168, f32[34,258,258]{2,1,0:T(8,128)} %get-tuple-element.201, s32[]{:T(128)S(6)} %add.207, s32[]{:T(128)S(6)} %add.208, s32[]{:T(128)S(6)} %select_n.9, ...), kind=kLoop, calls=%fused_computation.14.clone.1 | loop fusion | flops 7077888 | bytes 11534356 | tf_op jit(solution)/shard_map/while/body/eval_jaxpr/stack | solution.py:27
  159.3 1.0 copy-done
  161.2 1.1 fusion.33
  162.3 1.3 multiply_multiply_fusion.2
  163.6 1.6 fusion.34
  167.8 7.8 %multiply_bitcast_fusion.3 = (f32[1,4,256,256]{3,2,1,0:T(8,128)}, f32[4,256,256]{2,1,0:T(8,128)S(1)}) fusion(f32[34,258,258]{2,1,0:T(8,128)} %get-tuple-element.201, s32[]{:T(128)S(6)} %add.207, s32[]{:T(128)S(6)} %add.208, s32[]{:T(128)S(6)} %select_n.9, s32[]{:T(128)S(6)} %add.209, s32[]{:T(128)S(6)} %add.210), kind=kLoop, calls=%fused_computation.20.clone.1 | loop fusion | flops 6291456 | bytes 9437204 | tf_op jit(solution)/shard_map/while/body/eval_jaxpr/stack | solution.py:27
  175.6 7.0 %fusion.31 = (f32[1,4,256,256]{3,2,1,0:T(8,128)S(1)}, f32[1,4,256,256]{3,2,1,0:T(8,128)S(1)}, f32[4,256,256]{2,1,0:T(8,128)S(1)}) fusion(f32[4,256,256]{2,1,0:T(8,128)S(1)} %get-tuple-element.168, f32[34,258,258]{2,1,0:T(8,128)} %get-tuple-element.201, s32[]{:T(128)S(6)} %add.207, s32[]{:T(128)S(6)} %add.208, s32[]{:T(128)S(6)} %select_n.9, ...), kind=kLoop, calls=%fused_computation.14.clone.1 | loop fusion | flops 7077888 | bytes 11534356 | tf_op jit(solution)/shard_map/while/body/eval_jaxpr/stack | solution.py:27
  184.7 1.1 fusion.33
  185.8 1.3 multiply_multiply_fusion.2
  187.1 1.6 fusion.34
  191.2 7.8 %multiply_bitcast_fusion.3 = (f32[1,4,256,256]{3,2,1,0:T(8,128)}, f32[4,256,256]{2,1,0:T(8,128)S(1)}) fusion(f32[34,258,258]{2,1,0:T(8,128)} %get-tuple-element.201, s32[]{:T(128)S(6)} %add.207, s32[]{:T(128)S(6)} %add.208, s32[]{:T(128)S(6)} %select_n.9, s32[]{:T(128)S(6)} %add.209, s32[]{:T(128)S(6)} %add.210), kind=kLoop, calls=%fused_computation.20.clone.1 | loop fusion | flops 6291456 | bytes 9437204 | tf_op jit(solution)/shard_map/while/body/eval_jaxpr/stack | solution.py:27
  199.0 7.0 %fusion.31 = (f32[1,4,256,256]{3,2,1,0:T(8,128)S(1)}, f32[1,4,256,256]{3,2,1,0:T(8,128)S(1)}, f32[4,256,256]{2,1,0:T(8,128)S(1)}) fusion(f32[4,256,256]{2,1,0:T(8,128)S(1)} %get-tuple-element.168, f32[34,258,258]{2,1,0:T(8,128)} %get-tuple-element.201, s32[]{:T(128)S(6)} %add.207, s32[]{:T(128)S(6)} %add.208, s32[]{:T(128)S(6)} %select_n.9, ...), kind=kLoop, calls=%fused_computation.14.clone.1 | loop fusion | flops 7077888 | bytes 11534356 | tf_op jit(solution)/shard_map/while/body/eval_jaxpr/stack | solution.py:27
  208.1 1.1 fusion.33
  209.2 1.3 multiply_multiply_fusion.2
  210.5 1.6 fusion.34
  214.6 7.7 %multiply_bitcast_fusion.3 = (f32[1,4,256,256]{3,2,1,0:T(8,128)}, f32[4,256,256]{2,1,0:T(8,128)S(1)}) fusion(f32[34,258,258]{2,1,0:T(8,128)} %get-tuple-element.201, s32[]{:T(128)S(6)} %add.207, s32[]{:T(128)S(6)} %add.208, s32[]{:T(128)S(6)} %select_n.9, s32[]{:T(128)S(6)} %add.209, s32[]{:T(128)S(6)} %add.210), kind=kLoop, calls=%fused_computation.20.clone.1 | loop fusion | flops 6291456 | bytes 9437204 | tf_op jit(solution)/shard_map/while/body/eval_jaxpr/stack | solution.py:27
  222.3 6.9 %fusion.31 = (f32[1,4,256,256]{3,2,1,0:T(8,128)S(1)}, f32[1,4,256,256]{3,2,1,0:T(8,128)S(1)}, f32[4,256,256]{2,1,0:T(8,128)S(1)}) fusion(f32[4,256,256]{2,1,0:T(8,128)S(1)} %get-tuple-element.168, f32[34,258,258]{2,1,0:T(8,128)} %get-tuple-element.201, s32[]{:T(128)S(6)} %add.207, s32[]{:T(128)S(6)} %add.208, s32[]{:T(128)S(6)} %select_n.9, ...), kind=kLoop, calls=%fused_computation.14.clone.1 | loop fusion | flops 7077888 | bytes 11534356 | tf_op jit(solution)/shard_map/while/body/eval_jaxpr/stack | solution.py:27
  231.4 1.1 fusion.33
  232.4 1.3 multiply_multiply_fusion.2
  233.7 1.6 fusion.34
  237.9 8.2 %multiply_bitcast_fusion.3 = (f32[1,4,256,256]{3,2,1,0:T(8,128)}, f32[4,256,256]{2,1,0:T(8,128)S(1)}) fusion(f32[34,258,258]{2,1,0:T(8,128)} %get-tuple-element.201, s32[]{:T(128)S(6)} %add.207, s32[]{:T(128)S(6)} %add.208, s32[]{:T(128)S(6)} %select_n.9, s32[]{:T(128)S(6)} %add.209, s32[]{:T(128)S(6)} %add.210), kind=kLoop, calls=%fused_computation.20.clone.1 | loop fusion | flops 6291456 | bytes 9437204 | tf_op jit(solution)/shard_map/while/body/eval_jaxpr/stack | solution.py:27
  246.1 7.4 %fusion.31 = (f32[1,4,256,256]{3,2,1,0:T(8,128)S(1)}, f32[1,4,256,256]{3,2,1,0:T(8,128)S(1)}, f32[4,256,256]{2,1,0:T(8,128)S(1)}) fusion(f32[4,256,256]{2,1,0:T(8,128)S(1)} %get-tuple-element.168, f32[34,258,258]{2,1,0:T(8,128)} %get-tuple-element.201, s32[]{:T(128)S(6)} %add.207, s32[]{:T(128)S(6)} %add.208, s32[]{:T(128)S(6)} %select_n.9, ...), kind=kLoop, calls=%fused_computation.14.clone.1 | loop fusion | flops 7077888 | bytes 11534356 | tf_op jit(solution)/shard_map/while/body/eval_jaxpr/stack | solution.py:27
  255.6 1.1 fusion.33
  256.7 1.3 multiply_multiply_fusion.2
  258.0 1.6 fusion.34
  260.8 1.2 pad_maximum_fusion.1
  262.1 38.3 %all_to_all.5 = f32[4,16,16,256]{3,2,0,1:T(8,128)S(1)} all-to-all(f32[4,16,16,256]{3,2,0,1:T(8,128)S(1)} %copy.6), channel_id=1, replica_groups=mesh['gx'=4,'gy'=4,'gz'=16] {'gz'}, dimensions={1} | all-to-all | bytes 2097152 | tf_op jit(solution)/shard_map/all_to_all | solution.py:73
  (99 shorter events, 28.7 us)
Async XLA Ops:
  10.7 5.9 %collective-permute-start = (f32[32,256,1]{1,0,2:T(8,128)S(1)}, f32[32,256,1]{1,0,2:T(8,128)S(1)}, u32[]{:S(2)}, u32[]{:S(2)}) collective-permute-start(f32[32,256,1]{1,0,2:T(8,128)S(1)} %copy.7), channel_id=1, source_target_pairs={{0,64},{64,128},{128,192},{1,65},{65,129},{129,193},{2,66},{66,130... | collective-permute-start | bytes 98312 | tf_op jit(solution)/shard_map/ppermute | solution.py:12
  15.3 4.5 %collective-permute-start.1 = (f32[32,256,1]{1,0,2:T(8,128)S(1)}, f32[32,256,1]{1,0,2:T(8,128)S(1)}, u32[]{:S(2)}, u32[]{:S(2)}) collective-permute-start(f32[32,256,1]{1,0,2:T(8,128)S(1)} %copy.8), channel_id=1, source_target_pairs={{64,0},{128,64},{192,128},{65,1},{129,65},{193,129},{66,2},{130,66... | collective-permute-start | bytes 98312 | tf_op jit(solution)/shard_map/ppermute | solution.py:15
  22.4 11.4 %copy-start.1 = (f32[32,256,1]{2,1,0:T(8,128)S(1)}, f32[32,256,1]{2,1,0:T(8,128)}, u32[]{:S(2)}) copy-start(f32[32,256,1]{2,1,0:T(8,128)} %copy.4) | copy-start | bytes 98308
  22.4 11.4 %copy-start.2 = (f32[32,256,1]{2,1,0:T(8,128)S(1)}, f32[32,256,1]{2,1,0:T(8,128)}, u32[]{:S(2)}) copy-start(f32[32,256,1]{2,1,0:T(8,128)} %copy.5) | copy-start | bytes 98308
  24.2 5.4 %collective-permute-start.2 = (f32[32,1,258]{2,1,0:T(1,128)S(1)}, f32[32,1,258]{2,1,0:T(1,128)S(1)}, u32[]{:S(2)}, u32[]{:S(2)}) collective-permute-start(f32[32,1,258]{2,1,0:T(1,128)S(1)} %get-tuple-element.126), channel_id=1, source_target_pairs={{0,16},{16,32},{32,48},{1,17},{17,33},{33,49},{2,18},{18,34},{34,5... | collective-permute-start | bytes 99080 | tf_op jit(solution)/shard_map/ppermute | solution.py:12
  27.8 6.0 %collective-permute-start.3 = (f32[32,1,258]{2,1,0:T(1,128)S(1)}, f32[32,1,258]{2,1,0:T(1,128)S(1)}, u32[]{:S(2)}, u32[]{:S(2)}) collective-permute-start(f32[32,1,258]{2,1,0:T(1,128)S(1)} %get-tuple-element.127), channel_id=1, source_target_pairs={{16,0},{32,16},{48,32},{17,1},{33,17},{49,33},{18,2},{34,18},{50,3... | collective-permute-start | bytes 99080 | tf_op jit(solution)/shard_map/ppermute | solution.py:15
  35.2 13.9 %collective-permute-start.4 = (f32[1,258,258]{2,1,0:T(8,128)S(1)}, f32[1,258,258]{2,1,0:T(8,128)S(1)}, u32[]{:S(2)}, u32[]{:S(2)}) collective-permute-start(f32[1,258,258]{2,1,0:T(8,128)S(1)} %get-tuple-element.124), channel_id=1, source_target_pairs={{0,1},{1,2},{2,3},{3,4},{4,5},{5,6},{6,7},{7,8},{8,9},{9,10},{10,1... | collective-permute-start | bytes 798776 | tf_op jit(solution)/shard_map/ppermute | solution.py:12
  39.0 14.0 %collective-permute-start.5 = (f32[1,258,258]{2,1,0:T(8,128)S(1)}, f32[1,258,258]{2,1,0:T(8,128)S(1)}, u32[]{:S(2)}, u32[]{:S(2)}) collective-permute-start(f32[1,258,258]{2,1,0:T(8,128)S(1)} %get-tuple-element.125), channel_id=1, source_target_pairs={{1,0},{2,1},{3,2},{4,3},{5,4},{6,5},{7,6},{8,7},{9,8},{10,9},{11,1... | collective-permute-start | bytes 798776 | tf_op jit(solution)/shard_map/ppermute | solution.py:15
  89.0 1.0 copy-start
  90.9 4.0 %copy-start.3 = (f32[3,256,256]{2,1,0:T(8,128)S(1)}, f32[3,256,256]{2,1,0:T(8,128)}, u32[]{:S(2)}) copy-start(f32[3,256,256]{2,1,0:T(8,128)} %get-tuple-element.187) | copy-start | bytes 2359300 | tf_op jit(solution)/shard_map/while
  95.2 0.9 copy-start.4
  112.4 1.0 copy-start
  114.4 4.0 %copy-start.3 = (f32[3,256,256]{2,1,0:T(8,128)S(1)}, f32[3,256,256]{2,1,0:T(8,128)}, u32[]{:S(2)}) copy-start(f32[3,256,256]{2,1,0:T(8,128)} %get-tuple-element.187) | copy-start | bytes 2359300 | tf_op jit(solution)/shard_map/while
  118.6 0.9 copy-start.4
  135.8 1.0 copy-start
  137.7 4.0 %copy-start.3 = (f32[3,256,256]{2,1,0:T(8,128)S(1)}, f32[3,256,256]{2,1,0:T(8,128)}, u32[]{:S(2)}) copy-start(f32[3,256,256]{2,1,0:T(8,128)} %get-tuple-element.187) | copy-start | bytes 2359300 | tf_op jit(solution)/shard_map/while
  141.9 0.9 copy-start.4
  159.3 1.0 copy-start
  161.2 4.0 %copy-start.3 = (f32[3,256,256]{2,1,0:T(8,128)S(1)}, f32[3,256,256]{2,1,0:T(8,128)}, u32[]{:S(2)}) copy-start(f32[3,256,256]{2,1,0:T(8,128)} %get-tuple-element.187) | copy-start | bytes 2359300 | tf_op jit(solution)/shard_map/while
  165.5 0.9 copy-start.4
  182.8 1.0 copy-start
  184.7 4.0 %copy-start.3 = (f32[3,256,256]{2,1,0:T(8,128)S(1)}, f32[3,256,256]{2,1,0:T(8,128)}, u32[]{:S(2)}) copy-start(f32[3,256,256]{2,1,0:T(8,128)} %get-tuple-element.187) | copy-start | bytes 2359300 | tf_op jit(solution)/shard_map/while
  188.9 0.9 copy-start.4
  206.2 1.0 copy-start
  208.1 4.0 %copy-start.3 = (f32[3,256,256]{2,1,0:T(8,128)S(1)}, f32[3,256,256]{2,1,0:T(8,128)}, u32[]{:S(2)}) copy-start(f32[3,256,256]{2,1,0:T(8,128)} %get-tuple-element.187) | copy-start | bytes 2359300 | tf_op jit(solution)/shard_map/while
  212.3 0.9 copy-start.4
  229.4 1.0 copy-start
  231.4 4.0 %copy-start.3 = (f32[3,256,256]{2,1,0:T(8,128)S(1)}, f32[3,256,256]{2,1,0:T(8,128)}, u32[]{:S(2)}) copy-start(f32[3,256,256]{2,1,0:T(8,128)} %get-tuple-element.187) | copy-start | bytes 2359300 | tf_op jit(solution)/shard_map/while
  235.6 0.9 copy-start.4
  253.7 1.0 copy-start
  255.6 4.0 %copy-start.3 = (f32[3,256,256]{2,1,0:T(8,128)S(1)}, f32[3,256,256]{2,1,0:T(8,128)}, u32[]{:S(2)}) copy-start(f32[3,256,256]{2,1,0:T(8,128)} %get-tuple-element.187) | copy-start | bytes 2359300 | tf_op jit(solution)/shard_map/while
  259.9 0.9 copy-start.4
where the time goes:
time: 303 us; the launch traced here: 301 us
  other arithmetic  179 us (59%)
  local copies, waits for them, and re-layouts  46.8 us (15%)
  blocking collectives  38.3 us (13%)
  waiting for transfers between devices  16.9 us (6%)
  starting transfers between devices  14 us (5%)
  loops' own time  6.02 us (2%)
    another operation x16, other arithmetic, sample_light(): jnp.stack([jax.nn.sigmoid(2.0 * centre_slice) * shading, jnp.exp(-centre_...  119 us
    all_to_all x1, blocking collectives, per_device(): lax.all_to_all(tiled, 'gz', split_axis=1, concat_axis=1, tiled=True)  38.3 us
    concatenate x1, other arithmetic, padded_2(): block = jnp.concatenate([low, block, high], axis=dim)  19.6 us
    while x48, local copies, waits for them, and re-layouts  14.9 us
    reduce_sum x8, other arithmetic, march(): colour_sum = colour_sum + jnp.sum(weights[None] * emitted, axis=1)  13 us
    mul x8, other arithmetic, march(): weights = transmit[None] * before * opacity  10.2 us
    ppermute x3, starting transfers between devices, padded_2(): lax.ppermute(lax.slice_in_dim(block, block.shape[dim] - width, None, axis...  9.23 us
    mul x8, other arithmetic, march(): transmit = transmit * through[-1]  8.74 us
  transfers between devices with their start and end apart: 6, of which 5 were waited for; matrix products, arithmetic and copies ran while one was open for 2% of the time, Pallas kernels for 0%

commit v1 on v0

v1 whole, which is shorter than its diff:
```python
import jax
import jax.numpy as jnp
from jax import lax
from jax.experimental import pallas as pl
from jax.experimental.pallas import tpu as pltpu
from jax.sharding import PartitionSpec as P

LOG2E = 1.4426950408889634
LANES = 128


def face_kernel(f_ref, left_ref, right_ref, low_ref, high_ref, packed):
    step = pl.program_id(0)
    lane = lax.broadcasted_iota(jnp.int32, (8, LANES), 1)

    @pl.when(step == 0)
    def _():
        packed[...] = jnp.zeros_like(packed)

    def tile(r, carry):
        rows = pl.ds(pl.multiple_of(r * 8, 8), 8)
        acc = pltpu.roll(packed[rows, :], LANES - 8, 1)
        for kk in range(8):
            first = f_ref[kk, rows, 0:LANES]
            last = f_ref[kk, rows, LANES : 2 * LANES]
            acc = jnp.where(lane == 24 + kk, pltpu.roll(first, 24 + kk, 1), acc)
            acc = jnp.where(lane == 56 + kk, pltpu.roll(last, 57 + kk, 1), acc)
        packed[rows, :] = acc
        return carry

    lax.fori_loop(0, 32, tile, 0, unroll=4)
    for kk in range(8):
        low_ref[pl.ds(kk, 1), :] = f_ref[kk, 0:1, :]
        high_ref[pl.ds(kk, 1), :] = f_ref[kk, 255:256, :]

    @pl.when(step == pl.num_programs(0) - 1)
    def _():
        turned = packed[...].T
        left_ref[...] = turned[0:32]
        right_ref[...] = turned[32:64]


def faces(field):
    depth, rows, cols = field.shape
    face = jax.ShapeDtypeStruct((depth, rows), jnp.float32)
    return pl.pallas_call(
        face_kernel,
        grid=(depth // 8,),
        in_specs=[pl.BlockSpec((8, rows, cols), lambda i: (i, 0, 0))],
        out_specs=[
            pl.BlockSpec((depth, rows), lambda i: (0, 0)),
            pl.BlockSpec((depth, rows), lambda i: (0, 0)),
            pl.BlockSpec((8, cols), lambda i: (i, 0)),
            pl.BlockSpec((8, cols), lambda i: (i, 0)),
        ],
        out_shape=[face] * 4,
        scratch_shapes=[pltpu.VMEM((rows, LANES), jnp.float32)],
        compiler_params=pltpu.CompilerParams(vmem_limit_bytes=32 * 1024 * 1024),
    )(field)


def march_kernel(
    density, f_ref, left_ref, right_ref, low_ref, high_ref, near_ref, far_ref, out_ref, buf, mix, side, sems
):
    depth = f_ref.shape[0]
    parts = 4
    part_rows = 256 // parts

    def copy(part, half):
        return pltpu.make_async_copy(
            f_ref.at[:, pl.ds(part * part_rows, part_rows), pl.ds(half * LANES, LANES)],
            buf.at[half, :, pl.ds(8 + part * part_rows, part_rows), :],
            sems.at[part * 2 + half],
        )

    for part in range(parts):
        for half in range(2):
            copy(part, half).start()

    mix[...] = jnp.zeros_like(mix)
    for k in range(depth):
        mix[pl.ds(2 * k, 1), :] = left_ref[pl.ds(k, 1), :]
        mix[pl.ds((2 * k + LANES - 1) % LANES, 1), :] = right_ref[pl.ds(k, 1), :]
    side[...] = mix[...].T
    for k in range(depth):
        for half in range(2):
            cols = pl.ds(half * LANES, LANES)
            buf[half, k, pl.ds(7, 1), :] = low_ref[pl.ds(k, 1), cols]
            buf[half, k, pl.ds(264, 1), :] = high_ref[pl.ds(k, 1), cols]

    lane = lax.broadcasted_iota(jnp.int32, (8, LANES), 1)
    is_first = lane == 0
    is_last = lane == LANES - 1
    ext_scale = 4.0 * density * LOG2E
    ext_base = 1.2 * density * LOG2E

    def tile(r, carry):
        base = pl.multiple_of(r * 8, 8)
        here = pl.ds(8 + base, 8)
        edge = side[pl.ds(base, 8), :]
        prev = [near_ref[pl.ds(base, 8), pl.ds(h * LANES, LANES)] for h in range(2)]
        cur = [buf[h, 0, here, :] for h in range(2)]
        through = [jnp.ones((8, LANES), jnp.float32)] * 2
        total = [jnp.zeros((8, LANES), jnp.float32)] * 2
        tilted = [jnp.zeros((8, LANES), jnp.float32)] * 2
        bell = [jnp.zeros((8, LANES), jnp.float32)] * 2
        for k in range(depth):
            if k + 1 < depth:
                nxt = [buf[h, k + 1, here, :] for h in range(2)]
            else:
                nxt = [far_ref[pl.ds(base, 8), pl.ds(h * LANES, LANES)] for h in range(2)]
            fwd = [pltpu.roll(c, LANES - 1, 1) for c in cur]
            bwd = [pltpu.roll(c, 1, 1) for c in cur]
            upper = [jnp.where(is_last, fwd[1], fwd[0]), jnp.where(is_last, edge, fwd[1])]
            lower = [jnp.where(is_first, edge, bwd[0]), jnp.where(is_first, bwd[0], bwd[1])]
            if k + 1 < depth:
                edge = pltpu.roll(edge, LANES - 2, 1)
            for h in range(2):
                f = cur[h]
                a = upper[h] - lower[h]
                b = buf[h, k, pl.ds(base + 9, 8), :] - buf[h, k, pl.ds(base + 7, 8), :]
                c = nxt[h] - prev[h]
                bc = b + c
                slope = jnp.abs(a + (bc + bc))
                inv = lax.rsqrt((a * a + b * b) + (c * c + 4.0))
                t = jnp.tanh(f)
                gauss = jnp.exp2(f * (f * -LOG2E))
                keep = jnp.exp2((1.0 + t) * (inv * inv * ext_scale - ext_base))
                after = through[h] * keep
                w = through[h] - after
                ws = w * (1.0 + slope * inv)
                through[h] = after
                total[h] = total[h] + ws
                tilted[h] = tilted[h] + ws * t
                bell[h] = bell[h] + ws * gauss
            prev, cur = cur, nxt
        band = r // 2
        rows = pl.ds(pl.multiple_of((r % 2) * 8, 8), 8)
        for h in range(2):
            cols = pl.ds(h * LANES, LANES)
            out_ref[band, 0, rows, cols] = total[h]
            out_ref[band, 1, rows, cols] = tilted[h]
            out_ref[band, 2, rows, cols] = bell[h]
            out_ref[band, 3, rows, cols] = through[h]
        return carry

    tiles = part_rows // 8
    for half in range(2):
        copy(0, half).wait()
    for part in range(parts):
        if part + 1 < parts:
            for half in range(2):
                copy(part + 1, half).wait()
        lax.fori_loop(part * tiles, (part + 1) * tiles, tile, 0)


def march(field, left, right, low, high, near, far, density):
    depth, rows, cols = field.shape
    bands = 16
    vmem = pl.BlockSpec(memory_space=pltpu.VMEM)

    def kernel(*refs):
        march_kernel(density, *refs)

    return pl.pallas_call(
        kernel,
        in_specs=[pl.BlockSpec(memory_space=pl.ANY)] + [vmem] * 6,
        out_specs=vmem,
        out_shape=jax.ShapeDtypeStruct((bands, 4, rows // bands, cols), jnp.float32),
        scratch_shapes=[
            pltpu.VMEM((2, depth, rows + 16, LANES), jnp.float32),
            pltpu.VMEM((LANES, rows), jnp.float32),
            pltpu.VMEM((rows, LANES), jnp.float32),
            pltpu.SemaphoreType.DMA((8,)),
        ],
        compiler_params=pltpu.CompilerParams(vmem_limit_bytes=40 * 1024 * 1024),
    )(field, left, right, low, high, near, far)


def blend_kernel(parts_ref, out_ref):
    through = jnp.ones(parts_ref.shape[2:], jnp.float32)
    sums = [jnp.zeros(parts_ref.shape[2:], jnp.float32)] * 3
    for d in range(parts_ref.shape[0]):
        for c in range(3):
            sums[c] = sums[c] + through * parts_ref[d, c]
        through = through * parts_ref[d, 3]
    out_ref[0] = (sums[0] + sums[1]) * 0.125
    out_ref[1] = sums[2] * 0.25
    out_ref[2] = (sums[0] - sums[1]) * 0.125
    out_ref[3] = 1.0 - through


def blend(parts):
    return pl.pallas_call(
        blend_kernel,
        out_shape=jax.ShapeDtypeStruct(parts.shape[1:], jnp.float32),
    )(parts)


def shift(block, axis, up):
    count = lax.axis_size(axis)
    pairs = [(i, i + 1) if up else (i + 1, i) for i in range(count - 1)]
    return lax.ppermute(block, axis, pairs)


def per_device(field):
    depth = field.shape[0]
    density = 4.0 / (depth * lax.axis_size("gz"))
    near = shift(field[depth - 1], "gz", True)
    far = shift(field[0], "gz", False)
    left, right, low, high = faces(field)
    before_x = shift(right, "gx", True)
    after_x = shift(left, "gx", False)
    before_y = shift(high, "gy", True)
    after_y = shift(low, "gy", False)
    parts = march(field, before_x, after_x, before_y, after_y, near, far, density)
    parts = lax.all_to_all(parts, "gz", split_axis=0, concat_axis=0, tiled=True)
    return blend(parts)


def solution(mesh):
    return jax.shard_map(
        per_device,
        mesh=mesh,
        in_specs=(P("gz", "gy", "gx"),),
        out_specs=P(None, ("gy", "gz"), "gx"),
        check_vma=False,
    )
```

time: 303 us -> 140 us (0.46)
  other arithmetic: 179 us -> 0 us
  Pallas kernels: 0 us -> 75.7 us
  local copies, waits for them, and re-layouts: 46.8 us -> 4.44 us
  waiting for transfers between devices: 16.9 us -> 4.51 us
  loops' own time: 6.02 us -> 0 us
    another operation x24 -> x0, other arithmetic: 120 us -> none  [the longest x16 119 us: sample_light(): jnp.stack([jax.nn.sigmoid(2.0 * centre_slice) * shading, jnp.exp(-centre_...]
    pallas_call x0 -> x3, Pallas kernels: none -> 75.7 us  [the longest x1 69.1 us: march(): pl.pallas_call(kernel, in_specs=[pl.BlockSpec(memory_space=pl.ANY)] + [vm...]
    concatenate x2 -> x0, other arithmetic: 20.8 us -> none  [the longest x1 19.6 us: padded_2(): block = jnp.concatenate([low, block, high], axis=dim)]
    mul x20 -> x0, other arithmetic: 19 us -> none  [the longest x8 10.2 us: march(): weights = transmit[None] * before * opacity]
    slice x12 -> x0, local copies, waits for them, and re-layouts: 15.6 us -> none  [the longest x1 7.91 us: padded_2(): lax.slice_in_dim(block, block.shape[dim] - width, None, axis=dim)]
    while x48 -> x0, local copies, waits for them, and re-layouts: 14.9 us -> none
    reduce_sum x8 -> x0, other arithmetic: 13 us -> none  [march(): colour_sum = colour_sum + jnp.sum(weights[None] * emitted, axis=1)]
    ppermute x6, waiting for transfers between devices: 16.9 us -> 4.51 us  [shift(): return lax.ppermute(block, axis, pairs)]
  transfers between devices with their start and end apart: 6 -> 6, of which waited for: 5 -> 2; matrix products, arithmetic and copies ran while one was open for 2% -> 0% of each run, Pallas kernels for 0% -> 3%
where the time goes in v1:
time: 140 us; the launch traced here: 138 us
  Pallas kernels  75.7 us (54%)
  blocking collectives  40.3 us (29%)
  starting transfers between devices  13.2 us (9%)
  waiting for transfers between devices  4.51 us (3%)
  local copies, waits for them, and re-layouts  4.44 us (3%)
    pallas_call x1, Pallas kernels, march(): pl.pallas_call(kernel, in_specs=[pl.BlockSpec(memory_space=pl.ANY)] + [vm...  69.1 us
    all_to_all x1, blocking collectives, per_device(): parts = lax.all_to_all(parts, 'gz', split_axis=0, concat_axis=0, tiled=True)  40.3 us
    ppermute x6, starting transfers between devices, shift(): return lax.ppermute(block, axis, pairs)  13.2 us
    pallas_call x1, Pallas kernels, faces(): pl.pallas_call(face_kernel, grid=(depth // 8,), in_specs=[pl.BlockSpec((8...  4.65 us
    ppermute x6, waiting for transfers between devices, shift(): return lax.ppermute(block, axis, pairs)  4.51 us
    unnamed x4, local copies, waits for them, and re-layouts  3.38 us
  transfers between devices with their start and end apart: 6, of which 2 were waited for; matrix products, arithmetic and copies ran while one was open for 0% of the time, Pallas kernels for 3%

profile of v1, /device:TPU:32, one launch (start us, length us, event | category | flops | bytes accessed | tf_op | source)
XLA Modules:
  0.0 138.3 jit_solution(12935539430220849033)
XLA Ops:
  0.0 1.1 slice_bitcast_fusion
  1.1 3.8 %collective-permute-start.5 = (f32[256,256]{1,0:T(8,128)S(1)}, f32[256,256]{1,0:T(8,128)S(1)}, u32[]{:S(2)}, u32[]{:S(2)}) collective-permute-start(f32[256,256]{1,0:T(8,128)S(1)} %get-tuple-element.13), channel_id=1, source_target_pairs={{1,0},{2,1},{3,2},{4,3},{5,4},{6,5},{7,6},{8,7},{9,8},{10,9},{11,1... | collective-permute-start | bytes 786440 | tf_op jit(solution)/shard_map/ppermute | solution.py:203
  4.8 2.1 %collective-permute-start.4 = (f32[256,256]{1,0:T(8,128)S(1)}, f32[256,256]{1,0:T(8,128)S(1)}, u32[]{:S(2)}, u32[]{:S(2)}) collective-permute-start(f32[256,256]{1,0:T(8,128)S(1)} %get-tuple-element.14), channel_id=1, source_target_pairs={{0,1},{1,2},{2,3},{3,4},{4,5},{5,6},{6,7},{7,8},{8,9},{9,10},{10,1... | collective-permute-start | bytes 786440 | tf_op jit(solution)/shard_map/ppermute | solution.py:203
  6.9 0.0 copy-start
  6.9 3.4 %copy-done = f32[32,256,256]{2,1,0:T(8,128)S(1)} copy-done((f32[32,256,256]{2,1,0:T(8,128)S(1)}, f32[32,256,256]{2,1,0:T(8,128)}, u32[]{:S(2)}) %copy-start) | copy-done | bytes 8388632
  10.3 0.0 copy-start.1
  10.3 4.7 %shard_map.17 = (f32[32,256]{1,0:T(8,128)S(1)}, f32[32,256]{1,0:T(8,128)S(1)}, f32[32,256]{1,0:T(8,128)S(1)}, f32[32,256]{1,0:T(8,128)S(1)}) custom-call(f32[32,256,256]{2,1,0:T(8,128)S(1)} %copy-done), custom_call_target="tpu_custom_call" | custom-call | tf_op jit(solution)/shard_map/pallas_call | solution.py:46
  15.0 1.4 collective-permute-start
  16.3 1.3 collective-permute-start.1
  17.6 3.4 %collective-permute-start.2 = (f32[32,256]{1,0:T(8,128)S(1)}, f32[32,256]{1,0:T(8,128)S(1)}, u32[]{:S(2)}, u32[]{:S(2)}) collective-permute-start(f32[32,256]{1,0:T(8,128)S(1)} %get-tuple-element.11), channel_id=1, source_target_pairs={{0,16},{16,32},{32,48},{1,17},{17,33},{33,49},{2,18},{18,34},{34,5... | collective-permute-start | bytes 98312 | tf_op jit(solution)/shard_map/ppermute | solution.py:203
  21.1 0.0 collective-permute-done.refs_1_
  21.1 1.3 collective-permute-start.3
  22.4 0.0 collective-permute-done.1.refs_2_
  22.4 0.3 collective-permute-done.2.refs_3_
  22.6 4.2 %collective-permute-done.3.refs_4_ = f32[32,256]{1,0:T(8,128)S(1)} collective-permute-done((f32[32,256]{1,0:T(8,128)S(1)}, f32[32,256]{1,0:T(8,128)S(1)}, u32[]{:S(2)}, u32[]{:S(2)}) %collective-permute-start.3) | collective-permute-done | bytes 32800 | tf_op jit(solution)/shard_map/ppermute | solution.py:203
  26.9 0.0 collective-permute-done.5.refs_6_
  26.9 0.0 collective-permute-done.4.refs_5_
  26.9 0.0 copy-done.1
  26.9 69.1 %shard_map.18 = f32[16,4,16,256]{3,2,1,0:T(8,128)S(1)} custom-call(f32[32,256,256]{2,1,0:T(8,128)S(1)} %copy-done.1, f32[32,256]{1,0:T(8,128)S(1)} %collective-permute-done.refs_1_, f32[32,256]{1,0:T(8,128)S(1)} %collective-permute-done.1.refs_2_, f32[32,256]{1,0:T(8,128)S(1)} %collective-permute-done.2.refs_3_, ...), custom_call_target="tpu_custom_call" | custom-call | tf_op jit(solution)/shard_map/pallas_call | solution.py:165
  96.0 40.3 %all_to_all.5.parts_ref = f32[16,4,16,256]{3,2,1,0:T(8,128)} all-to-all(f32[16,4,16,256]{3,2,1,0:T(8,128)S(1)} %shard_map.18), channel_id=1, replica_groups=mesh['gx'=4,'gy'=4,'gz'=16] {'gz'}, dimensions={0} | all-to-all | bytes 2097152 | tf_op jit(solution)/shard_map/all_to_all | solution.py:217
  136.3 1.9 %shard_map.19 = f32[4,16,256]{2,1,0:T(8,128)} custom-call(f32[16,4,16,256]{3,2,1,0:T(8,128)} %all_to_all.5.parts_ref), custom_call_target="tpu_custom_call" | custom-call | tf_op jit(solution)/shard_map/pallas_call | solution.py:194
Async XLA Ops:
  1.1 25.8 %collective-permute-start.5 = (f32[256,256]{1,0:T(8,128)S(1)}, f32[256,256]{1,0:T(8,128)S(1)}, u32[]{:S(2)}, u32[]{:S(2)}) collective-permute-start(f32[256,256]{1,0:T(8,128)S(1)} %get-tuple-element.13), channel_id=1, source_target_pairs={{1,0},{2,1},{3,2},{4,3},{5,4},{6,5},{7,6},{8,7},{9,8},{10,9},{11,1... | collective-permute-start | bytes 786440 | tf_op jit(solution)/shard_map/ppermute | solution.py:203
  4.8 22.0 %collective-permute-start.4 = (f32[256,256]{1,0:T(8,128)S(1)}, f32[256,256]{1,0:T(8,128)S(1)}, u32[]{:S(2)}, u32[]{:S(2)}) collective-permute-start(f32[256,256]{1,0:T(8,128)S(1)} %get-tuple-element.14), channel_id=1, source_target_pairs={{0,1},{1,2},{2,3},{3,4},{4,5},{5,6},{6,7},{7,8},{8,9},{9,10},{10,1... | collective-permute-start | bytes 786440 | tf_op jit(solution)/shard_map/ppermute | solution.py:203
  6.9 3.4 %copy-start = (f32[32,256,256]{2,1,0:T(8,128)S(1)}, f32[32,256,256]{2,1,0:T(8,128)}, u32[]{:S(2)}) copy-start(f32[32,256,256]{2,1,0:T(8,128)} %refs_0_.1) | copy-start | bytes 25165828
  10.3 16.6 %copy-start.1 = (f32[32,256,256]{2,1,0:T(8,128)S(1)}, f32[32,256,256]{2,1,0:T(8,128)}, u32[]{:S(2)}) copy-start(f32[32,256,256]{2,1,0:T(8,128)} %refs_0_.1) | copy-start | bytes 25165828
  15.0 6.1 %collective-permute-start = (f32[32,256]{1,0:T(8,128)S(1)}, f32[32,256]{1,0:T(8,128)S(1)}, u32[]{:S(2)}, u32[]{:S(2)}) collective-permute-start(f32[32,256]{1,0:T(8,128)S(1)} %get-tuple-element.9), channel_id=1, source_target_pairs={{0,64},{64,128},{128,192},{1,65},{65,129},{129,193},{2,66},{66,130... | collective-permute-start | bytes 98312 | tf_op jit(solution)/shard_map/ppermute | solution.py:203
  16.3 6.0 %collective-permute-start.1 = (f32[32,256]{1,0:T(8,128)S(1)}, f32[32,256]{1,0:T(8,128)S(1)}, u32[]{:S(2)}, u32[]{:S(2)}) collective-permute-start(f32[32,256]{1,0:T(8,128)S(1)} %get-tuple-element.10), channel_id=1, source_target_pairs={{64,0},{128,64},{192,128},{65,1},{129,65},{193,129},{66,2},{130,66... | collective-permute-start | bytes 98312 | tf_op jit(solution)/shard_map/ppermute | solution.py:203
  17.6 5.0 %collective-permute-start.2 = (f32[32,256]{1,0:T(8,128)S(1)}, f32[32,256]{1,0:T(8,128)S(1)}, u32[]{:S(2)}, u32[]{:S(2)}) collective-permute-start(f32[32,256]{1,0:T(8,128)S(1)} %get-tuple-element.11), channel_id=1, source_target_pairs={{0,16},{16,32},{32,48},{1,17},{17,33},{33,49},{2,18},{18,34},{34,5... | collective-permute-start | bytes 98312 | tf_op jit(solution)/shard_map/ppermute | solution.py:203
  21.1 5.8 %collective-permute-start.3 = (f32[32,256]{1,0:T(8,128)S(1)}, f32[32,256]{1,0:T(8,128)S(1)}, u32[]{:S(2)}, u32[]{:S(2)}) collective-permute-start(f32[32,256]{1,0:T(8,128)S(1)} %get-tuple-element.12), channel_id=1, source_target_pairs={{16,0},{32,16},{48,32},{17,1},{33,17},{49,33},{18,2},{34,18},{50,3... | collective-permute-start | bytes 98312 | tf_op jit(solution)/shard_map/ppermute | solution.py:203

commit v2 on v1

--- a/solution.py
+++ b/solution.py
@@ -55,7 +55,7 @@
         ],
         out_shape=[face] * 4,
         scratch_shapes=[pltpu.VMEM((rows, LANES), jnp.float32)],
-        compiler_params=pltpu.CompilerParams(vmem_limit_bytes=32 * 1024 * 1024),
+        compiler_params=pltpu.CompilerParams(vmem_limit_bytes=60 * 1024 * 1024),
     )(field)
 
 
@@ -97,7 +97,7 @@
     def tile(r, carry):
         base = pl.multiple_of(r * 8, 8)
         here = pl.ds(8 + base, 8)
-        edge = side[pl.ds(base, 8), :]
+        packed = side[pl.ds(base, 8), :]
         prev = [near_ref[pl.ds(base, 8), pl.ds(h * LANES, LANES)] for h in range(2)]
         cur = [buf[h, 0, here, :] for h in range(2)]
         through = [jnp.ones((8, LANES), jnp.float32)] * 2
@@ -111,10 +111,9 @@
                 nxt = [far_ref[pl.ds(base, 8), pl.ds(h * LANES, LANES)] for h in range(2)]
             fwd = [pltpu.roll(c, LANES - 1, 1) for c in cur]
             bwd = [pltpu.roll(c, 1, 1) for c in cur]
+            edge = pltpu.roll(packed, LANES - 2 * k, 1) if k else packed
             upper = [jnp.where(is_last, fwd[1], fwd[0]), jnp.where(is_last, edge, fwd[1])]
             lower = [jnp.where(is_first, edge, bwd[0]), jnp.where(is_first, bwd[0], bwd[1])]
-            if k + 1 < depth:
-                edge = pltpu.roll(edge, LANES - 2, 1)
             for h in range(2):
                 f = cur[h]
                 a = upper[h] - lower[h]
@@ -173,7 +172,7 @@
             pltpu.VMEM((rows, LANES), jnp.float32),
             pltpu.SemaphoreType.DMA((8,)),
         ],
-        compiler_params=pltpu.CompilerParams(vmem_limit_bytes=40 * 1024 * 1024),
+        compiler_params=pltpu.CompilerParams(vmem_limit_bytes=60 * 1024 * 1024),
     )(field, left, right, low, high, near, far)
 
 

time: 140 us -> 88 us (0.63)
  the two profiles are of different devices: /device:TPU:32 before, /device:TPU:1 now
where the time goes in v2:
time: 88 us; the launch traced here: 87.5 us
  blocking collectives  39.4 us (45%)
  Pallas kernels  25.2 us (29%)
  starting transfers between devices  16.8 us (19%)
  waiting for transfers between devices  3.54 us (4%)
  local copies, waits for them, and re-layouts  2.46 us (3%)
    all_to_all x1, blocking collectives, per_device(): parts = lax.all_to_all(parts, 'gz', split_axis=0, concat_axis=0, tiled=True)  39.4 us
    ppermute x6, starting transfers between devices, shift(): return lax.ppermute(block, axis, pairs)  16.8 us
    pallas_call x1, Pallas kernels, march(): pl.pallas_call(kernel, in_specs=[pl.BlockSpec(memory_space=pl.ANY)] + [vm...  15.8 us
    pallas_call x1, Pallas kernels, faces(): pl.pallas_call(face_kernel, grid=(depth // 8,), in_specs=[pl.BlockSpec((8...  7.47 us
    ppermute x6, waiting for transfers between devices, shift(): return lax.ppermute(block, axis, pairs)  3.54 us
    pallas_call x1, Pallas kernels, blend(): pl.pallas_call(blend_kernel, out_shape=jax.ShapeDtypeStruct(parts.shape[1...  1.93 us
  transfers between devices with their start and end apart: 6, of which 1 were waited for; matrix products, arithmetic and copies ran while one was open for 0% of the time, Pallas kernels for 9%

profile of v2, /device:TPU:1, one launch (start us, length us, event | category | flops | bytes accessed | tf_op | source)
XLA Modules:
  0.0 87.5 jit_solution(11744795961586077442)
XLA Ops:
  0.0 1.1 %slice_bitcast_fusion = (f32[256,256]{1,0:T(8,128)S(1)}, f32[256,256]{1,0:T(8,128)S(1)}) fusion(f32[32,256,256]{2,1,0:T(8,128)} %refs_0_.1), kind=kLoop, calls=%fused_computation | loop fusion | bytes 1048576 | tf_op jit(solution)/shard_map/squeeze | solution.py:209
  1.1 1.3 %collective-permute-start.5 = (f32[256,256]{1,0:T(8,128)S(1)}, f32[256,256]{1,0:T(8,128)S(1)}, u32[]{:S(2)}, u32[]{:S(2)}) collective-permute-start(f32[256,256]{1,0:T(8,128)S(1)} %get-tuple-element.13), channel_id=1, source_target_pairs={{1,0},{2,1},{3,2},{4,3},{5,4},{6,5},{7,6},{8,7},{9,8},{10,9},{11,1... | collective-permute-start | bytes 786440 | tf_op jit(solution)/shard_map/ppermute | solution.py:202
  2.4 5.0 %collective-permute-start.4 = (f32[256,256]{1,0:T(8,128)S(1)}, f32[256,256]{1,0:T(8,128)S(1)}, u32[]{:S(2)}, u32[]{:S(2)}) collective-permute-start(f32[256,256]{1,0:T(8,128)S(1)} %get-tuple-element.14), channel_id=1, source_target_pairs={{0,1},{1,2},{2,3},{3,4},{4,5},{5,6},{6,7},{7,8},{8,9},{9,10},{10,1... | collective-permute-start | bytes 786440 | tf_op jit(solution)/shard_map/ppermute | solution.py:202
  7.4 7.5 %shard_map.17 = (f32[32,256]{1,0:T(8,128)}, f32[32,256]{1,0:T(8,128)}, f32[32,256]{1,0:T(8,128)}, f32[32,256]{1,0:T(8,128)}) custom-call(f32[32,256,256]{2,1,0:T(8,128)} %refs_0_.1), custom_call_target="tpu_custom_call" | custom-call | tf_op jit(solution)/shard_map/pallas_call | solution.py:46
  14.9 4.1 %collective-permute-start = (f32[32,256]{1,0:T(8,128)}, f32[32,256]{1,0:T(8,128)S(1)}, u32[]{:S(2)}, u32[]{:S(2)}) collective-permute-start(f32[32,256]{1,0:T(8,128)} %get-tuple-element.9), channel_id=1, source_target_pairs={{0,64},{64,128},{128,192},{1,65},{65,129},{129,193},{2,66},{66,130... | collective-permute-start | bytes 98312 | tf_op jit(solution)/shard_map/ppermute | solution.py:202
  19.0 1.9 %collective-permute-start.1 = (f32[32,256]{1,0:T(8,128)}, f32[32,256]{1,0:T(8,128)S(1)}, u32[]{:S(2)}, u32[]{:S(2)}) collective-permute-start(f32[32,256]{1,0:T(8,128)} %get-tuple-element.10), channel_id=1, source_target_pairs={{64,0},{128,64},{192,128},{65,1},{129,65},{193,129},{66,2},{130,66... | collective-permute-start | bytes 98312 | tf_op jit(solution)/shard_map/ppermute | solution.py:202
  20.9 3.1 %collective-permute-start.2 = (f32[32,256]{1,0:T(8,128)}, f32[32,256]{1,0:T(8,128)S(1)}, u32[]{:S(2)}, u32[]{:S(2)}) collective-permute-start(f32[32,256]{1,0:T(8,128)} %get-tuple-element.11), channel_id=1, source_target_pairs={{0,16},{16,32},{32,48},{1,17},{17,33},{33,49},{2,18},{18,34},{34,5... | collective-permute-start | bytes 98312 | tf_op jit(solution)/shard_map/ppermute | solution.py:202
  24.1 0.0 collective-permute-done.refs_1_
  24.1 0.0 copy-start.2
  24.1 1.3 %collective-permute-start.3 = (f32[32,256]{1,0:T(8,128)}, f32[32,256]{1,0:T(8,128)S(1)}, u32[]{:S(2)}, u32[]{:S(2)}) collective-permute-start(f32[32,256]{1,0:T(8,128)} %get-tuple-element.12), channel_id=1, source_target_pairs={{16,0},{32,16},{48,32},{17,1},{33,17},{49,33},{18,2},{34,18},{50,3... | collective-permute-start | bytes 98312 | tf_op jit(solution)/shard_map/ppermute | solution.py:202
  25.4 0.0 collective-permute-done.1.refs_2_
  25.4 0.0 copy-start.3
  25.4 0.0 collective-permute-done.2.refs_3_
  25.4 0.0 copy-start.4
  25.4 3.5 %collective-permute-done.3.refs_4_ = f32[32,256]{1,0:T(8,128)S(1)} collective-permute-done((f32[32,256]{1,0:T(8,128)}, f32[32,256]{1,0:T(8,128)S(1)}, u32[]{:S(2)}, u32[]{:S(2)}) %collective-permute-start.3) | collective-permute-done | bytes 32800 | tf_op jit(solution)/shard_map/ppermute | solution.py:202
  29.0 0.0 copy-start.5
  29.0 0.0 collective-permute-done.5.refs_6_
  29.0 0.0 copy-start
  29.0 0.0 collective-permute-done.4.refs_5_
  29.0 0.0 copy-done.2
  29.0 0.0 copy-done.3
  29.0 0.0 copy-done.4
  29.0 0.6 copy-done.5
  29.6 0.1 copy-done
  29.7 0.0 copy-start.1
  29.7 0.7 copy-done.1
  30.4 15.8 %shard_map.18 = f32[16,4,16,256]{3,2,1,0:T(8,128)} custom-call(f32[32,256,256]{2,1,0:T(8,128)} %refs_0_.1, f32[32,256]{1,0:T(8,128)} %copy-done.2, f32[32,256]{1,0:T(8,128)} %copy-done.3, f32[32,256]{1,0:T(8,128)} %copy-done.4, f32[32,256]{1,0:T(8,128)} %copy-done.5, f32[256,256]{1,0:T(8,128)} %copy-done.1, f32[256,256]{1,0:T(8,128)} %copy-done), custom_call_target="tpu_custom_call" | custom-call | tf_op jit(solution)/shard_map/pallas_call | solution.py:164
  46.2 39.4 %all_to_all.5.parts_ref = f32[16,4,16,256]{3,2,1,0:T(8,128)} all-to-all(f32[16,4,16,256]{3,2,1,0:T(8,128)} %shard_map.18), channel_id=1, replica_groups=mesh['gx'=4,'gy'=4,'gz'=16] {'gz'}, dimensions={0} | all-to-all | bytes 2097152 | tf_op jit(solution)/shard_map/all_to_all | solution.py:216
  85.6 1.9 %shard_map.19 = f32[4,16,256]{2,1,0:T(8,128)} custom-call(f32[16,4,16,256]{3,2,1,0:T(8,128)} %all_to_all.5.parts_ref), custom_call_target="tpu_custom_call" | custom-call | tf_op jit(solution)/shard_map/pallas_call | solution.py:193
Async XLA Ops:
  1.1 27.9 %collective-permute-start.5 = (f32[256,256]{1,0:T(8,128)S(1)}, f32[256,256]{1,0:T(8,128)S(1)}, u32[]{:S(2)}, u32[]{:S(2)}) collective-permute-start(f32[256,256]{1,0:T(8,128)S(1)} %get-tuple-element.13), channel_id=1, source_target_pairs={{1,0},{2,1},{3,2},{4,3},{5,4},{6,5},{7,6},{8,7},{9,8},{10,9},{11,1... | collective-permute-start | bytes 786440 | tf_op jit(solution)/shard_map/ppermute | solution.py:202
  2.4 26.6 %collective-permute-start.4 = (f32[256,256]{1,0:T(8,128)S(1)}, f32[256,256]{1,0:T(8,128)S(1)}, u32[]{:S(2)}, u32[]{:S(2)}) collective-permute-start(f32[256,256]{1,0:T(8,128)S(1)} %get-tuple-element.14), channel_id=1, source_target_pairs={{0,1},{1,2},{2,3},{3,4},{4,5},{5,6},{6,7},{7,8},{8,9},{9,10},{10,1... | collective-permute-start | bytes 786440 | tf_op jit(solution)/shard_map/ppermute | solution.py:202
  14.9 9.2 %collective-permute-start = (f32[32,256]{1,0:T(8,128)}, f32[32,256]{1,0:T(8,128)S(1)}, u32[]{:S(2)}, u32[]{:S(2)}) collective-permute-start(f32[32,256]{1,0:T(8,128)} %get-tuple-element.9), channel_id=1, source_target_pairs={{0,64},{64,128},{128,192},{1,65},{65,129},{129,193},{2,66},{66,130... | collective-permute-start | bytes 98312 | tf_op jit(solution)/shard_map/ppermute | solution.py:202
  19.0 6.4 %collective-permute-start.1 = (f32[32,256]{1,0:T(8,128)}, f32[32,256]{1,0:T(8,128)S(1)}, u32[]{:S(2)}, u32[]{:S(2)}) collective-permute-start(f32[32,256]{1,0:T(8,128)} %get-tuple-element.10), channel_id=1, source_target_pairs={{64,0},{128,64},{192,128},{65,1},{129,65},{193,129},{66,2},{130,66... | collective-permute-start | bytes 98312 | tf_op jit(solution)/shard_map/ppermute | solution.py:202
  20.9 4.5 %collective-permute-start.2 = (f32[32,256]{1,0:T(8,128)}, f32[32,256]{1,0:T(8,128)S(1)}, u32[]{:S(2)}, u32[]{:S(2)}) collective-permute-start(f32[32,256]{1,0:T(8,128)} %get-tuple-element.11), channel_id=1, source_target_pairs={{0,16},{16,32},{32,48},{1,17},{17,33},{33,49},{2,18},{18,34},{34,5... | collective-permute-start | bytes 98312 | tf_op jit(solution)/shard_map/ppermute | solution.py:202
  24.1 4.9 %copy-start.2 = (f32[32,256]{1,0:T(8,128)}, f32[32,256]{1,0:T(8,128)S(1)}, u32[]{:S(2)}) copy-start(f32[32,256]{1,0:T(8,128)S(1)} %collective-permute-done.refs_1_) | copy-start | bytes 98308
  24.1 4.9 %collective-permute-start.3 = (f32[32,256]{1,0:T(8,128)}, f32[32,256]{1,0:T(8,128)S(1)}, u32[]{:S(2)}, u32[]{:S(2)}) collective-permute-start(f32[32,256]{1,0:T(8,128)} %get-tuple-element.12), channel_id=1, source_target_pairs={{16,0},{32,16},{48,32},{17,1},{33,17},{49,33},{18,2},{34,18},{50,3... | collective-permute-start | bytes 98312 | tf_op jit(solution)/shard_map/ppermute | solution.py:202
  25.4 3.6 %copy-start.3 = (f32[32,256]{1,0:T(8,128)}, f32[32,256]{1,0:T(8,128)S(1)}, u32[]{:S(2)}) copy-start(f32[32,256]{1,0:T(8,128)S(1)} %collective-permute-done.1.refs_2_) | copy-start | bytes 98308
  25.4 3.6 %copy-start.4 = (f32[32,256]{1,0:T(8,128)}, f32[32,256]{1,0:T(8,128)S(1)}, u32[]{:S(2)}) copy-start(f32[32,256]{1,0:T(8,128)S(1)} %collective-permute-done.2.refs_3_) | copy-start | bytes 98308
  29.0 0.6 copy-start.5
  29.0 0.7 copy-start
  29.7 0.7 copy-start.1

commit v3 on v2

v3 whole, which is shorter than its diff:
```python
import jax
import jax.numpy as jnp
from jax import lax
from jax.experimental import pallas as pl
from jax.experimental.pallas import tpu as pltpu
from jax.sharding import PartitionSpec as P

LOG2E = 1.4426950408889634
LANES = 128
PARTS = 8
FACE_LIMIT = 40 * 1024 * 1024
MARCH_LIMIT = 24 * 1024 * 1024


def is_even(axis):
    return lax.rem(lax.axis_index(axis), 2) == 0


def pick(even, yes, no):
    return jnp.where(jnp.broadcast_to(even, yes.shape), yes, no)


def face_kernel(f_ref, out_ref, x0_ref, x1_ref, y0_ref, y1_ref, z0_ref, z1_ref, packed, sems):
    depth, rows, cols = f_ref.shape
    part_rows = rows // PARTS
    lane = lax.broadcasted_iota(jnp.int32, (8, LANES), 1)

    def copy(part, half):
        span = pl.ds(pl.multiple_of(part * part_rows, 8), part_rows)
        return pltpu.make_async_copy(
            f_ref.at[:, span, pl.ds(half * LANES, LANES)], out_ref.at[half, :, span, :], sems.at[part * 2 + half]
        )

    for part in range(PARTS):
        for half in range(2):
            copy(part, half).start()

    def tile(r):
        here = pl.ds(pl.multiple_of(r * 8, 8), 8)
        acc = jnp.zeros((8, LANES), jnp.float32)
        for k in range(depth):
            first = pltpu.roll(out_ref[0, k, here, :], k, 1) if k else out_ref[0, k, here, :]
            last = pltpu.roll(out_ref[1, k, here, :], depth + k + 1, 1)
            acc = jnp.where(lane == k, first, acc)
            acc = jnp.where(lane == depth + k, last, acc)
        packed[here, :] = acc

    def step(part, carry):
        for half in range(2):
            copy(part, half).wait()
        for r in range(part_rows // 8):
            tile(part * (part_rows // 8) + r)
        return carry

    lax.fori_loop(0, PARTS, step, 0)
    even_x, even_y, even_z = is_even("gx"), is_even("gy"), is_even("gz")
    turned = packed[...].T
    left, right = turned[0:depth], turned[depth : 2 * depth]
    x0_ref[...] = pick(even_x, right, left)
    x1_ref[...] = pick(even_x, left, right)
    for half in range(2):
        for k in range(depth):
            low, high = out_ref[half, k, 0:1, :], out_ref[half, k, rows - 1 : rows, :]
            y0_ref[half, pl.ds(k, 1), :] = pick(even_y, high, low)
            y1_ref[half, pl.ds(k, 1), :] = pick(even_y, low, high)
        near, far = out_ref[half, 0], out_ref[half, depth - 1]
        z0_ref[half] = pick(even_z, far, near)
        z1_ref[half] = pick(even_z, near, far)


def faces(field):
    depth, rows, cols = field.shape
    vmem = pl.BlockSpec(memory_space=pltpu.VMEM)
    shapes = [(2, depth, rows, LANES)] + [(depth, rows)] * 2 + [(2, depth, LANES)] * 2 + [(2, rows, LANES)] * 2
    return pl.pallas_call(
        face_kernel,
        in_specs=[pl.BlockSpec(memory_space=pl.ANY)],
        out_specs=[vmem] * 7,
        out_shape=[jax.ShapeDtypeStruct(shape, jnp.float32) for shape in shapes],
        scratch_shapes=[pltpu.VMEM((rows, LANES), jnp.float32), pltpu.SemaphoreType.DMA((2 * PARTS,))],
        compiler_params=pltpu.CompilerParams(vmem_limit_bytes=FACE_LIMIT),
    )(field)


def march_kernel(density, f_ref, x0_ref, x1_ref, y0_ref, y1_ref, z0_ref, z1_ref, out_ref, rim, mix, side):
    depth, rows = f_ref.shape[1:3]
    even_x, even_y, even_z = is_even("gx"), is_even("gy"), is_even("gz")
    mix[...] = jnp.zeros_like(mix)
    for k in range(depth):
        first, second = x0_ref[pl.ds(k, 1), :], x1_ref[pl.ds(k, 1), :]
        mix[pl.ds(2 * k, 1), :] = pick(even_x, second, first)
        mix[pl.ds((2 * k + LANES - 1) % LANES, 1), :] = pick(even_x, first, second)
    side[...] = mix[...].T
    for half in range(2):
        for k in range(depth):
            first, second = y0_ref[half, pl.ds(k, 1), :], y1_ref[half, pl.ds(k, 1), :]
            rim[0, half, k, pl.ds(7, 1), :] = pick(even_y, second, first)
            rim[0, half, k, pl.ds(8, 16), :] = f_ref[half, k, pl.ds(0, 16), :]
            rim[1, half, k, pl.ds(0, 16), :] = f_ref[half, k, pl.ds(rows - 16, 16), :]
            rim[1, half, k, pl.ds(16, 1), :] = pick(even_y, first, second)

    lane = lax.broadcasted_iota(jnp.int32, (8, LANES), 1)
    is_first = lane == 0
    is_last = lane == LANES - 1
    ext_scale = 4.0 * density * LOG2E
    ext_base = 1.2 * density * LOG2E

    def tile(r, source, offset):
        base = pl.multiple_of(r * 8, 8)

        def load(half, k, up):
            return source[half, k, pl.ds(offset + up, 8), :]

        def depth_halo(half, yes, no):
            return pick(even_z, yes[half, pl.ds(base, 8), :], no[half, pl.ds(base, 8), :])

        packed = side[pl.ds(base, 8), :]
        prev = [depth_halo(h, z1_ref, z0_ref) for h in range(2)]
        cur = [load(h, 0, 0) for h in range(2)]
        through = [jnp.ones((8, LANES), jnp.float32)] * 2
        total = [jnp.zeros((8, LANES), jnp.float32)] * 2
        tilted = [jnp.zeros((8, LANES), jnp.float32)] * 2
        bell = [jnp.zeros((8, LANES), jnp.float32)] * 2
        for k in range(depth):
            if k + 1 < depth:
                nxt = [load(h, k + 1, 0) for h in range(2)]
            else:
                nxt = [depth_halo(h, z0_ref, z1_ref) for h in range(2)]
            edge = pltpu.roll(packed, LANES - 2 * k, 1) if k else packed
            fwd = [pltpu.roll(c, LANES - 1, 1) for c in cur]
            bwd = [pltpu.roll(c, 1, 1) for c in cur]
            upper = [jnp.where(is_last, fwd[1], fwd[0]), jnp.where(is_last, edge, fwd[1])]
            lower = [jnp.where(is_first, edge, bwd[0]), jnp.where(is_first, bwd[0], bwd[1])]
            for h in range(2):
                f = cur[h]
                a = upper[h] - lower[h]
                b = load(h, k, 1) - load(h, k, -1)
                c = nxt[h] - prev[h]
                bc = b + c
                slope = jnp.abs(a + (bc + bc))
                inv = lax.rsqrt((a * a + b * b) + (c * c + 4.0))
                t = jnp.tanh(f)
                gauss = jnp.exp2(f * (f * -LOG2E))
                keep = jnp.exp2((1.0 + t) * (inv * inv * ext_scale - ext_base))
                after = through[h] * keep
                w = through[h] - after
                ws = w * (1.0 + slope * inv)
                through[h] = after
                total[h] = total[h] + ws
                tilted[h] = tilted[h] + ws * t
                bell[h] = bell[h] + ws * gauss
            prev, cur = cur, nxt
        band = r // 2
        target = pl.ds(pl.multiple_of(lax.rem(r, 2) * 8, 8), 8)
        for h in range(2):
            cols = pl.ds(h * LANES, LANES)
            out_ref[band, 0, target, cols] = total[h]
            out_ref[band, 1, target, cols] = tilted[h]
            out_ref[band, 2, target, cols] = bell[h]
            out_ref[band, 3, target, cols] = through[h]

    def inner(r, carry):
        tile(r, f_ref, r * 8)
        return carry

    tile(jnp.int32(0), rim.at[0], 8)
    lax.fori_loop(1, rows // 8 - 1, inner, 0)
    tile(jnp.int32(rows // 8 - 1), rim.at[1], 8)


def march(halos, density):
    depth, rows = halos[0].shape[1:3]
    cols = 2 * LANES
    bands = 16
    vmem = pl.BlockSpec(memory_space=pltpu.VMEM)

    def kernel(*refs):
        march_kernel(density, *refs)

    return pl.pallas_call(
        kernel,
        in_specs=[vmem] * 7,
        out_specs=vmem,
        out_shape=jax.ShapeDtypeStruct((bands, 4, rows // bands, cols), jnp.float32),
        scratch_shapes=[
            pltpu.VMEM((2, 2, depth, 24, LANES), jnp.float32),
            pltpu.VMEM((LANES, rows), jnp.float32),
            pltpu.VMEM((rows, LANES), jnp.float32),
        ],
        compiler_params=pltpu.CompilerParams(vmem_limit_bytes=MARCH_LIMIT),
    )(*halos)


def blend_kernel(parts_ref, out_ref):
    through = jnp.ones(parts_ref.shape[2:], jnp.float32)
    sums = [jnp.zeros(parts_ref.shape[2:], jnp.float32)] * 3
    for d in range(parts_ref.shape[0]):
        for c in range(3):
            sums[c] = sums[c] + through * parts_ref[d, c]
        through = through * parts_ref[d, 3]
    out_ref[0] = (sums[0] + sums[1]) * 0.125
    out_ref[1] = sums[2] * 0.25
    out_ref[2] = (sums[0] - sums[1]) * 0.125
    out_ref[3] = 1.0 - through


def blend(parts):
    return pl.pallas_call(
        blend_kernel,
        out_shape=jax.ShapeDtypeStruct(parts.shape[1:], jnp.float32),
    )(parts)


def swap(block, axis, start):
    pairs = []
    for i in range(start, lax.axis_size(axis) - 1, 2):
        pairs += [(i, i + 1), (i + 1, i)]
    return lax.ppermute(block, axis, pairs)


def per_device(field):
    depth = field.shape[0]
    density = 4.0 / (depth * lax.axis_size("gz"))
    whole, x0, x1, y0, y1, z0, z1 = faces(field)
    z0, z1 = swap(z0, "gz", 0), swap(z1, "gz", 1)
    x0, x1 = swap(x0, "gx", 0), swap(x1, "gx", 1)
    y0, y1 = swap(y0, "gy", 0), swap(y1, "gy", 1)
    parts = march((whole, x0, x1, y0, y1, z0, z1), density)
    parts = lax.all_to_all(parts, "gz", split_axis=0, concat_axis=0, tiled=True)
    return blend(parts)


def solution(mesh):
    return jax.shard_map(
        per_device,
        mesh=mesh,
        in_specs=(P("gz", "gy", "gx"),),
        out_specs=P(None, ("gy", "gz"), "gx"),
        check_vma=False,
    )
```

time: 88 us -> 70.2 us (0.80)
  the two profiles are of different devices: /device:TPU:1 before, /device:TPU:4 now
where the time goes in v3:
time: 70.2 us; the launch traced here: 69.9 us
  blocking collectives  41.5 us (59%)
  Pallas kernels  17.9 us (25%)
  starting transfers between devices  6.62 us (9%)
  waiting for transfers between devices  3.88 us (6%)
    all_to_all x1, blocking collectives, per_device(): parts = lax.all_to_all(parts, 'gz', split_axis=0, concat_axis=0, tiled=True)  41.5 us
    pallas_call x1, Pallas kernels, march(): pl.pallas_call(kernel, in_specs=[vmem] * 7, out_specs=vmem, out_shape=jax...  11.8 us
    ppermute x6, starting transfers between devices, swap(): return lax.ppermute(block, axis, pairs)  6.62 us
    pallas_call x1, Pallas kernels, faces(): pl.pallas_call(face_kernel, in_specs=[pl.BlockSpec(memory_space=pl.ANY)],...  4.17 us
    ppermute x6, waiting for transfers between devices, swap(): return lax.ppermute(block, axis, pairs)  3.88 us
    pallas_call x1, Pallas kernels, blend(): pl.pallas_call(blend_kernel, out_shape=jax.ShapeDtypeStruct(parts.shape[1...  1.93 us
  transfers between devices with their start and end apart: 6, of which 2 were waited for; matrix products, arithmetic and copies ran while one was open for 0% of the time, Pallas kernels for 0%

profile of v3, /device:TPU:4, one launch (start us, length us, event | category | flops | bytes accessed | tf_op | source)
XLA Modules:
  0.0 69.9 jit_solution(5110602176542730952)
XLA Ops:
  0.0 4.2 %shard_map.17 = (f32[2,32,256,128]{3,2,1,0:T(8,128)S(1)}, f32[32,256]{1,0:T(8,128)S(1)}, f32[32,256]{1,0:T(8,128)S(1)}, f32[2,32,128]{2,1,0:T(8,128)S(1)}, f32[2...) custom-call(f32[32,256,256]{2,1,0:T(8,128)} %f_ref.1), custom_call_target="tpu_custom_call" | custom-call | tf_op jit(solution)/shard_map/pallas_call | solution.py:75
  4.2 2.0 %collective-permute-start.4 = (f32[2,256,128]{2,1,0:T(8,128)S(1)}, f32[2,256,128]{2,1,0:T(8,128)S(1)}, u32[]{:S(2)}, u32[]{:S(2)}) collective-permute-start(f32[2,256,128]{2,1,0:T(8,128)S(1)} %get-tuple-element.17), channel_id=1, source_target_pairs={{0,1},{1,0},{2,3},{3,2},{4,5},{5,4},{6,7},{7,6},{8,9},{9,8},{10,11... | collective-permute-start | bytes 786440 | tf_op jit(solution)/shard_map/ppermute | solution.py:218
  6.2 0.7 collective-permute-start.5
  6.9 0.1 collective-permute-start
  7.0 0.7 collective-permute-start.1
  7.6 1.3 %collective-permute-start.2 = (f32[2,32,128]{2,1,0:T(8,128)S(1)}, f32[2,32,128]{2,1,0:T(8,128)S(1)}, u32[]{:S(2)}, u32[]{:S(2)}) collective-permute-start(f32[2,32,128]{2,1,0:T(8,128)S(1)} %get-tuple-element.15), channel_id=1, source_target_pairs={{0,16},{16,0},{32,48},{48,32},{1,17},{17,1},{33,49},{49,33},{2,18}... | collective-permute-start | bytes 98312 | tf_op jit(solution)/shard_map/ppermute | solution.py:218
  8.9 0.0 collective-permute-done.refs_1_
  8.9 1.9 %collective-permute-start.3 = (f32[2,32,128]{2,1,0:T(8,128)S(1)}, f32[2,32,128]{2,1,0:T(8,128)S(1)}, u32[]{:S(2)}, u32[]{:S(2)}) collective-permute-start(f32[2,32,128]{2,1,0:T(8,128)S(1)} %get-tuple-element.16), channel_id=1, source_target_pairs={{16,32},{32,16},{17,33},{33,17},{18,34},{34,18},{19,35},{35,19},{2... | collective-permute-start | bytes 98312 | tf_op jit(solution)/shard_map/ppermute | solution.py:218
  10.8 0.0 collective-permute-done.1.refs_2_
  10.8 0.8 %collective-permute-done.2.refs_3_ = f32[2,32,128]{2,1,0:T(8,128)S(1)} collective-permute-done((f32[2,32,128]{2,1,0:T(8,128)S(1)}, f32[2,32,128]{2,1,0:T(8,128)S(1)}, u32[]{:S(2)}, u32[]{:S(2)}) %collective-permute-start.2) | collective-permute-done | bytes 32800 | tf_op jit(solution)/shard_map/ppermute | solution.py:218
  11.6 3.1 %collective-permute-done.3.refs_4_ = f32[2,32,128]{2,1,0:T(8,128)S(1)} collective-permute-done((f32[2,32,128]{2,1,0:T(8,128)S(1)}, f32[2,32,128]{2,1,0:T(8,128)S(1)}, u32[]{:S(2)}, u32[]{:S(2)}) %collective-permute-start.3) | collective-permute-done | bytes 32800 | tf_op jit(solution)/shard_map/ppermute | solution.py:218
  14.7 0.0 collective-permute-done.4.refs_5_
  14.7 0.0 collective-permute-done.5.refs_6_
  14.7 11.8 %shard_map.18 = f32[16,4,16,256]{3,2,1,0:T(8,128)S(1)} custom-call(f32[2,32,256,128]{3,2,1,0:T(8,128)S(1)} %get-tuple-element.12.refs_0_, f32[32,256]{1,0:T(8,128)S(1)} %collective-permute-done.refs_1_, f32[32,256]{1,0:T(8,128)S(1)} %collective-permute-done.1.refs_2_, f32[2,32,128]{2,1,0:T(8,128)S(1)} %collective-permute-done.2.refs_3_, ...), custom_call_target="tpu_custom_call" | custom-call | tf_op jit(solution)/shard_map/pallas_call | solution.py:180
  26.5 41.5 %all_to_all.5.parts_ref = f32[16,4,16,256]{3,2,1,0:T(8,128)} all-to-all(f32[16,4,16,256]{3,2,1,0:T(8,128)S(1)} %shard_map.18), channel_id=1, replica_groups=mesh['gx'=4,'gy'=4,'gz'=16] {'gz'}, dimensions={0} | all-to-all | bytes 2097152 | tf_op jit(solution)/shard_map/all_to_all | solution.py:229
  68.0 1.9 %shard_map.19 = f32[4,16,256]{2,1,0:T(8,128)} custom-call(f32[16,4,16,256]{3,2,1,0:T(8,128)} %all_to_all.5.parts_ref), custom_call_target="tpu_custom_call" | custom-call | tf_op jit(solution)/shard_map/pallas_call | solution.py:208
Async XLA Ops:
  4.2 10.5 %collective-permute-start.4 = (f32[2,256,128]{2,1,0:T(8,128)S(1)}, f32[2,256,128]{2,1,0:T(8,128)S(1)}, u32[]{:S(2)}, u32[]{:S(2)}) collective-permute-start(f32[2,256,128]{2,1,0:T(8,128)S(1)} %get-tuple-element.17), channel_id=1, source_target_pairs={{0,1},{1,0},{2,3},{3,2},{4,5},{5,4},{6,7},{7,6},{8,9},{9,8},{10,11... | collective-permute-start | bytes 786440 | tf_op jit(solution)/shard_map/ppermute | solution.py:218
  6.2 8.5 %collective-permute-start.5 = (f32[2,256,128]{2,1,0:T(8,128)S(1)}, f32[2,256,128]{2,1,0:T(8,128)S(1)}, u32[]{:S(2)}, u32[]{:S(2)}) collective-permute-start(f32[2,256,128]{2,1,0:T(8,128)S(1)} %get-tuple-element.18), channel_id=1, source_target_pairs={{1,2},{2,1},{3,4},{4,3},{5,6},{6,5},{7,8},{8,7},{9,10},{10,9},{11,... | collective-permute-start | bytes 786440 | tf_op jit(solution)/shard_map/ppermute | solution.py:218
  6.9 2.1 %collective-permute-start = (f32[32,256]{1,0:T(8,128)S(1)}, f32[32,256]{1,0:T(8,128)S(1)}, u32[]{:S(2)}, u32[]{:S(2)}) collective-permute-start(f32[32,256]{1,0:T(8,128)S(1)} %get-tuple-element.13), channel_id=1, source_target_pairs={{0,64},{64,0},{128,192},{192,128},{1,65},{65,1},{129,193},{193,129... | collective-permute-start | bytes 98312 | tf_op jit(solution)/shard_map/ppermute | solution.py:218
  7.0 3.9 %collective-permute-start.1 = (f32[32,256]{1,0:T(8,128)S(1)}, f32[32,256]{1,0:T(8,128)S(1)}, u32[]{:S(2)}, u32[]{:S(2)}) collective-permute-start(f32[32,256]{1,0:T(8,128)S(1)} %get-tuple-element.14), channel_id=1, source_target_pairs={{64,128},{128,64},{65,129},{129,65},{66,130},{130,66},{67,131},{13... | collective-permute-start | bytes 98312 | tf_op jit(solution)/shard_map/ppermute | solution.py:218
  7.6 4.0 %collective-permute-start.2 = (f32[2,32,128]{2,1,0:T(8,128)S(1)}, f32[2,32,128]{2,1,0:T(8,128)S(1)}, u32[]{:S(2)}, u32[]{:S(2)}) collective-permute-start(f32[2,32,128]{2,1,0:T(8,128)S(1)} %get-tuple-element.15), channel_id=1, source_target_pairs={{0,16},{16,0},{32,48},{48,32},{1,17},{17,1},{33,49},{49,33},{2,18}... | collective-permute-start | bytes 98312 | tf_op jit(solution)/shard_map/ppermute | solution.py:218
  8.9 5.8 %collective-permute-start.3 = (f32[2,32,128]{2,1,0:T(8,128)S(1)}, f32[2,32,128]{2,1,0:T(8,128)S(1)}, u32[]{:S(2)}, u32[]{:S(2)}) collective-permute-start(f32[2,32,128]{2,1,0:T(8,128)S(1)} %get-tuple-element.16), channel_id=1, source_target_pairs={{16,32},{32,16},{17,33},{33,17},{18,34},{34,18},{19,35},{35,19},{2... | collective-permute-start | bytes 98312 | tf_op jit(solution)/shard_map/ppermute | solution.py:218

commit v4 on v3

--- a/solution.py
+++ b/solution.py
@@ -14,6 +14,15 @@
 
 def is_even(axis):
     return lax.rem(lax.axis_index(axis), 2) == 0
+
+
+def at_end(axis):
+    place = lax.axis_index(axis)
+    return (place == 0) | (place == lax.axis_size(axis) - 1)
+
+
+def drop(end, block):
+    return jnp.where(jnp.broadcast_to(end, block.shape), 0.0, block)
 
 
 def pick(even, yes, no):
@@ -85,15 +94,16 @@
 def march_kernel(density, f_ref, x0_ref, x1_ref, y0_ref, y1_ref, z0_ref, z1_ref, out_ref, rim, mix, side):
     depth, rows = f_ref.shape[1:3]
     even_x, even_y, even_z = is_even("gx"), is_even("gy"), is_even("gz")
+    end_x, end_y, end_z = at_end("gx"), at_end("gy"), at_end("gz")
     mix[...] = jnp.zeros_like(mix)
     for k in range(depth):
-        first, second = x0_ref[pl.ds(k, 1), :], x1_ref[pl.ds(k, 1), :]
+        first, second = x0_ref[pl.ds(k, 1), :], drop(end_x, x1_ref[pl.ds(k, 1), :])
         mix[pl.ds(2 * k, 1), :] = pick(even_x, second, first)
         mix[pl.ds((2 * k + LANES - 1) % LANES, 1), :] = pick(even_x, first, second)
     side[...] = mix[...].T
     for half in range(2):
         for k in range(depth):
-            first, second = y0_ref[half, pl.ds(k, 1), :], y1_ref[half, pl.ds(k, 1), :]
+            first, second = y0_ref[half, pl.ds(k, 1), :], drop(end_y, y1_ref[half, pl.ds(k, 1), :])
             rim[0, half, k, pl.ds(7, 1), :] = pick(even_y, second, first)
             rim[0, half, k, pl.ds(8, 16), :] = f_ref[half, k, pl.ds(0, 16), :]
             rim[1, half, k, pl.ds(0, 16), :] = f_ref[half, k, pl.ds(rows - 16, 16), :]
@@ -111,11 +121,13 @@
         def load(half, k, up):
             return source[half, k, pl.ds(offset + up, 8), :]
 
-        def depth_halo(half, yes, no):
-            return pick(even_z, yes[half, pl.ds(base, 8), :], no[half, pl.ds(base, 8), :])
+        def depth_halo(half, near):
+            first = z0_ref[half, pl.ds(base, 8), :]
+            second = drop(end_z, z1_ref[half, pl.ds(base, 8), :])
+            return pick(even_z, second, first) if near else pick(even_z, first, second)
 
         packed = side[pl.ds(base, 8), :]
-        prev = [depth_halo(h, z1_ref, z0_ref) for h in range(2)]
+        prev = [depth_halo(h, True) for h in range(2)]
         cur = [load(h, 0, 0) for h in range(2)]
         through = [jnp.ones((8, LANES), jnp.float32)] * 2
         total = [jnp.zeros((8, LANES), jnp.float32)] * 2
@@ -125,7 +137,7 @@
             if k + 1 < depth:
                 nxt = [load(h, k + 1, 0) for h in range(2)]
             else:
-                nxt = [depth_halo(h, z0_ref, z1_ref) for h in range(2)]
+                nxt = [depth_halo(h, False) for h in range(2)]
             edge = pltpu.roll(packed, LANES - 2 * k, 1) if k else packed
             fwd = [pltpu.roll(c, LANES - 1, 1) for c in cur]
             bwd = [pltpu.roll(c, 1, 1) for c in cur]
@@ -137,8 +149,8 @@
                 b = load(h, k, 1) - load(h, k, -1)
                 c = nxt[h] - prev[h]
                 bc = b + c
-                slope = jnp.abs(a + (bc + bc))
-                inv = lax.rsqrt((a * a + b * b) + (c * c + 4.0))
+                slope = jnp.abs((bc + bc) + a)
+                inv = lax.rsqrt(((c * c + b * b) + 4.0) + a * a)
                 t = jnp.tanh(f)
                 gauss = jnp.exp2(f * (f * -LOG2E))
                 keep = jnp.exp2((1.0 + t) * (inv * inv * ext_scale - ext_base))
@@ -164,7 +176,7 @@
         return carry
 
     tile(jnp.int32(0), rim.at[0], 8)
-    lax.fori_loop(1, rows // 8 - 1, inner, 0)
+    lax.fori_loop(1, rows // 8 - 1, inner, 0, unroll=3)
     tile(jnp.int32(rows // 8 - 1), rim.at[1], 8)
 
 
@@ -212,9 +224,10 @@
 
 
 def swap(block, axis, start):
+    count = lax.axis_size(axis)
     pairs = []
-    for i in range(start, lax.axis_size(axis) - 1, 2):
-        pairs += [(i, i + 1), (i + 1, i)]
+    for i in range(start, count, 2):
+        pairs += [(i, (i + 1) % count), ((i + 1) % count, i)]
     return lax.ppermute(block, axis, pairs)
 
 

time: 70.2 us -> 65.7 us (0.936)
  the two profiles are of different devices: /device:TPU:4 before, /device:TPU:32 now
where the time goes in v4:
time: 65.7 us; the launch traced here: 65.3 us
  blocking collectives  36.4 us (55%)
  Pallas kernels  16.7 us (25%)
  starting transfers between devices  9.2 us (14%)
  waiting for transfers between devices  3.04 us (5%)
    all_to_all x1, blocking collectives, per_device(): parts = lax.all_to_all(parts, 'gz', split_axis=0, concat_axis=0, tiled=True)  36.4 us
    pallas_call x1, Pallas kernels, march(): pl.pallas_call(kernel, in_specs=[vmem] * 7, out_specs=vmem, out_shape=jax...  10.6 us
    ppermute x6, starting transfers between devices, swap(): return lax.ppermute(block, axis, pairs)  9.2 us
    pallas_call x1, Pallas kernels, faces(): pl.pallas_call(face_kernel, in_specs=[pl.BlockSpec(memory_space=pl.ANY)],...  4.17 us
    ppermute x6, waiting for transfers between devices, swap(): return lax.ppermute(block, axis, pairs)  3.04 us
    pallas_call x1, Pallas kernels, blend(): pl.pallas_call(blend_kernel, out_shape=jax.ShapeDtypeStruct(parts.shape[1...  1.93 us
  transfers between devices with their start and end apart: 6, of which 2 were waited for; matrix products, arithmetic and copies ran while one was open for 0% of the time, Pallas kernels for 0%

profile of v4, /device:TPU:32, one launch (start us, length us, event | category | flops | bytes accessed | tf_op | source)
XLA Modules:
  0.0 65.3 jit_solution(6502922636052688236)
XLA Ops:
  0.0 4.2 %shard_map.17 = (f32[2,32,256,128]{3,2,1,0:T(8,128)S(1)}, f32[32,256]{1,0:T(8,128)S(1)}, f32[32,256]{1,0:T(8,128)S(1)}, f32[2,32,128]{2,1,0:T(8,128)S(1)}, f32[2...) custom-call(f32[32,256,256]{2,1,0:T(8,128)} %f_ref.1), custom_call_target="tpu_custom_call" | custom-call | tf_op jit(solution)/shard_map/pallas_call | solution.py:84
  4.2 1.9 %collective-permute-start.4 = (f32[2,256,128]{2,1,0:T(8,128)S(1)}, f32[2,256,128]{2,1,0:T(8,128)S(1)}, u32[]{:S(2)}, u32[]{:S(2)}) collective-permute-start(f32[2,256,128]{2,1,0:T(8,128)S(1)} %get-tuple-element.17), channel_id=1, source_target_pairs={{0,1},{1,0},{2,3},{3,2},{4,5},{5,4},{6,7},{7,6},{8,9},{9,8},{10,11... | collective-permute-start | bytes 786440 | tf_op jit(solution)/shard_map/ppermute | solution.py:231
  6.1 2.0 %collective-permute-start.5 = (f32[2,256,128]{2,1,0:T(8,128)S(1)}, f32[2,256,128]{2,1,0:T(8,128)S(1)}, u32[]{:S(2)}, u32[]{:S(2)}) collective-permute-start(f32[2,256,128]{2,1,0:T(8,128)S(1)} %get-tuple-element.18), channel_id=1, source_target_pairs={{1,2},{2,1},{3,4},{4,3},{5,6},{6,5},{7,8},{8,7},{9,10},{10,9},{11,... | collective-permute-start | bytes 786440 | tf_op jit(solution)/shard_map/ppermute | solution.py:231
  8.1 0.0 collective-permute-start
  8.1 1.7 %collective-permute-start.1 = (f32[32,256]{1,0:T(8,128)S(1)}, f32[32,256]{1,0:T(8,128)S(1)}, u32[]{:S(2)}, u32[]{:S(2)}) collective-permute-start(f32[32,256]{1,0:T(8,128)S(1)} %get-tuple-element.14), channel_id=1, source_target_pairs={{64,128},{128,64},{192,0},{0,192},{65,129},{129,65},{193,1},{1,193... | collective-permute-start | bytes 98312 | tf_op jit(solution)/shard_map/ppermute | solution.py:231
  9.8 1.5 %collective-permute-start.2 = (f32[2,32,128]{2,1,0:T(8,128)S(1)}, f32[2,32,128]{2,1,0:T(8,128)S(1)}, u32[]{:S(2)}, u32[]{:S(2)}) collective-permute-start(f32[2,32,128]{2,1,0:T(8,128)S(1)} %get-tuple-element.15), channel_id=1, source_target_pairs={{0,16},{16,0},{32,48},{48,32},{1,17},{17,1},{33,49},{49,33},{2,18}... | collective-permute-start | bytes 98312 | tf_op jit(solution)/shard_map/ppermute | solution.py:231
  11.3 0.0 collective-permute-done.refs_1_
  11.3 2.1 %collective-permute-start.3 = (f32[2,32,128]{2,1,0:T(8,128)S(1)}, f32[2,32,128]{2,1,0:T(8,128)S(1)}, u32[]{:S(2)}, u32[]{:S(2)}) collective-permute-start(f32[2,32,128]{2,1,0:T(8,128)S(1)} %get-tuple-element.16), channel_id=1, source_target_pairs={{16,32},{32,16},{48,0},{0,48},{17,33},{33,17},{49,1},{1,49},{18,34... | collective-permute-start | bytes 98312 | tf_op jit(solution)/shard_map/ppermute | solution.py:231
  13.4 0.0 collective-permute-done.1.refs_2_
  13.4 0.3 collective-permute-done.2.refs_3_
  13.7 2.7 %collective-permute-done.3.refs_4_ = f32[2,32,128]{2,1,0:T(8,128)S(1)} collective-permute-done((f32[2,32,128]{2,1,0:T(8,128)S(1)}, f32[2,32,128]{2,1,0:T(8,128)S(1)}, u32[]{:S(2)}, u32[]{:S(2)}) %collective-permute-start.3) | collective-permute-done | bytes 32800 | tf_op jit(solution)/shard_map/ppermute | solution.py:231
  16.4 0.0 collective-permute-done.4.refs_5_
  16.4 0.0 collective-permute-done.5.refs_6_
  16.4 10.6 %shard_map.18 = f32[16,4,16,256]{3,2,1,0:T(8,128)S(1)} custom-call(f32[2,32,256,128]{3,2,1,0:T(8,128)S(1)} %get-tuple-element.12.refs_0_, f32[32,256]{1,0:T(8,128)S(1)} %collective-permute-done.refs_1_, f32[32,256]{1,0:T(8,128)S(1)} %collective-permute-done.1.refs_2_, f32[2,32,128]{2,1,0:T(8,128)S(1)} %collective-permute-done.2.refs_3_, ...), custom_call_target="tpu_custom_call" | custom-call | tf_op jit(solution)/shard_map/pallas_call | solution.py:192
  27.0 36.4 %all_to_all.5.parts_ref = f32[16,4,16,256]{3,2,1,0:T(8,128)} all-to-all(f32[16,4,16,256]{3,2,1,0:T(8,128)S(1)} %shard_map.18), channel_id=1, replica_groups=mesh['gx'=4,'gy'=4,'gz'=16] {'gz'}, dimensions={0} | all-to-all | bytes 2097152 | tf_op jit(solution)/shard_map/all_to_all | solution.py:242
  63.3 1.9 %shard_map.19 = f32[4,16,256]{2,1,0:T(8,128)} custom-call(f32[16,4,16,256]{3,2,1,0:T(8,128)} %all_to_all.5.parts_ref), custom_call_target="tpu_custom_call" | custom-call | tf_op jit(solution)/shard_map/pallas_call | solution.py:220
Async XLA Ops:
  4.2 12.2 %collective-permute-start.4 = (f32[2,256,128]{2,1,0:T(8,128)S(1)}, f32[2,256,128]{2,1,0:T(8,128)S(1)}, u32[]{:S(2)}, u32[]{:S(2)}) collective-permute-start(f32[2,256,128]{2,1,0:T(8,128)S(1)} %get-tuple-element.17), channel_id=1, source_target_pairs={{0,1},{1,0},{2,3},{3,2},{4,5},{5,4},{6,7},{7,6},{8,9},{9,8},{10,11... | collective-permute-start | bytes 786440 | tf_op jit(solution)/shard_map/ppermute | solution.py:231
  6.1 10.3 %collective-permute-start.5 = (f32[2,256,128]{2,1,0:T(8,128)S(1)}, f32[2,256,128]{2,1,0:T(8,128)S(1)}, u32[]{:S(2)}, u32[]{:S(2)}) collective-permute-start(f32[2,256,128]{2,1,0:T(8,128)S(1)} %get-tuple-element.18), channel_id=1, source_target_pairs={{1,2},{2,1},{3,4},{4,3},{5,6},{6,5},{7,8},{8,7},{9,10},{10,9},{11,... | collective-permute-start | bytes 786440 | tf_op jit(solution)/shard_map/ppermute | solution.py:231
  8.1 3.2 %collective-permute-start = (f32[32,256]{1,0:T(8,128)S(1)}, f32[32,256]{1,0:T(8,128)S(1)}, u32[]{:S(2)}, u32[]{:S(2)}) collective-permute-start(f32[32,256]{1,0:T(8,128)S(1)} %get-tuple-element.13), channel_id=1, source_target_pairs={{0,64},{64,0},{128,192},{192,128},{1,65},{65,1},{129,193},{193,129... | collective-permute-start | bytes 98312 | tf_op jit(solution)/shard_map/ppermute | solution.py:231
  8.1 5.3 %collective-permute-start.1 = (f32[32,256]{1,0:T(8,128)S(1)}, f32[32,256]{1,0:T(8,128)S(1)}, u32[]{:S(2)}, u32[]{:S(2)}) collective-permute-start(f32[32,256]{1,0:T(8,128)S(1)} %get-tuple-element.14), channel_id=1, source_target_pairs={{64,128},{128,64},{192,0},{0,192},{65,129},{129,65},{193,1},{1,193... | collective-permute-start | bytes 98312 | tf_op jit(solution)/shard_map/ppermute | solution.py:231
  9.8 3.9 %collective-permute-start.2 = (f32[2,32,128]{2,1,0:T(8,128)S(1)}, f32[2,32,128]{2,1,0:T(8,128)S(1)}, u32[]{:S(2)}, u32[]{:S(2)}) collective-permute-start(f32[2,32,128]{2,1,0:T(8,128)S(1)} %get-tuple-element.15), channel_id=1, source_target_pairs={{0,16},{16,0},{32,48},{48,32},{1,17},{17,1},{33,49},{49,33},{2,18}... | collective-permute-start | bytes 98312 | tf_op jit(solution)/shard_map/ppermute | solution.py:231
  11.3 5.1 %collective-permute-start.3 = (f32[2,32,128]{2,1,0:T(8,128)S(1)}, f32[2,32,128]{2,1,0:T(8,128)S(1)}, u32[]{:S(2)}, u32[]{:S(2)}) collective-permute-start(f32[2,32,128]{2,1,0:T(8,128)S(1)} %get-tuple-element.16), channel_id=1, source_target_pairs={{16,32},{32,16},{48,0},{0,48},{17,33},{33,17},{49,1},{1,49},{18,34... | collective-permute-start | bytes 98312 | tf_op jit(solution)/shard_map/ppermute | solution.py:231

commit v5 on v4

v5 whole, which is shorter than its diff:
```python
import functools

import jax
import jax.numpy as jnp
from jax import lax
from jax.experimental import pallas as pl
from jax.experimental.pallas import tpu as pltpu
from jax.sharding import PartitionSpec as P

LOG2E = 1.4426950408889634
LANES = 128
BANDS = 16
PARTS = 8
FACE_LIMIT = 40 * 1024 * 1024
MARCH_LIMIT = 24 * 1024 * 1024


def is_even(axis):
    return lax.rem(lax.axis_index(axis), 2) == 0


def at_end(axis):
    place = lax.axis_index(axis)
    return (place == 0) | (place == lax.axis_size(axis) - 1)


def drop(end, block):
    return jnp.where(jnp.broadcast_to(end, block.shape), 0.0, block)


def pick(even, yes, no):
    return jnp.where(jnp.broadcast_to(even, yes.shape), yes, no)


def face_kernel(f_ref, out_ref, x0_ref, x1_ref, y0_ref, y1_ref, z0_ref, z1_ref, packed, sems):
    depth, rows, cols = f_ref.shape
    part_rows = rows // PARTS
    lane = lax.broadcasted_iota(jnp.int32, (8, LANES), 1)

    def copy(part, half):
        span = pl.ds(pl.multiple_of(part * part_rows, 8), part_rows)
        return pltpu.make_async_copy(
            f_ref.at[:, span, pl.ds(half * LANES, LANES)], out_ref.at[half, :, span, :], sems.at[part * 2 + half]
        )

    for part in range(PARTS):
        for half in range(2):
            copy(part, half).start()

    def tile(r):
        here = pl.ds(pl.multiple_of(r * 8, 8), 8)
        acc = jnp.zeros((8, LANES), jnp.float32)
        for k in range(depth):
            first = pltpu.roll(out_ref[0, k, here, :], k, 1) if k else out_ref[0, k, here, :]
            last = pltpu.roll(out_ref[1, k, here, :], depth + k + 1, 1)
            acc = jnp.where(lane == k, first, acc)
            acc = jnp.where(lane == depth + k, last, acc)
        packed[here, :] = acc

    def step(part, carry):
        for half in range(2):
            copy(part, half).wait()
        for r in range(part_rows // 8):
            tile(part * (part_rows // 8) + r)
        return carry

    lax.fori_loop(0, PARTS, step, 0)
    even_x, even_y, even_z = is_even("gx"), is_even("gy"), is_even("gz")
    turned = packed[...].T
    left, right = turned[0:depth], turned[depth : 2 * depth]
    x0_ref[...] = pick(even_x, right, left)
    x1_ref[...] = pick(even_x, left, right)
    for half in range(2):
        for k in range(depth):
            low, high = out_ref[half, k, 0:1, :], out_ref[half, k, rows - 1 : rows, :]
            y0_ref[half, pl.ds(k, 1), :] = pick(even_y, high, low)
            y1_ref[half, pl.ds(k, 1), :] = pick(even_y, low, high)
        near, far = out_ref[half, 0], out_ref[half, depth - 1]
        z0_ref[half] = pick(even_z, far, near)
        z1_ref[half] = pick(even_z, near, far)


def faces(field):
    depth, rows, cols = field.shape
    vmem = pl.BlockSpec(memory_space=pltpu.VMEM)
    shapes = [(2, depth, rows, LANES)] + [(depth, rows)] * 2 + [(2, depth, LANES)] * 2 + [(2, rows, LANES)] * 2
    return pl.pallas_call(
        face_kernel,
        in_specs=[pl.BlockSpec(memory_space=pl.ANY)],
        out_specs=[vmem] * 7,
        out_shape=[jax.ShapeDtypeStruct(shape, jnp.float32) for shape in shapes],
        scratch_shapes=[pltpu.VMEM((rows, LANES), jnp.float32), pltpu.SemaphoreType.DMA((2 * PARTS,))],
        compiler_params=pltpu.CompilerParams(vmem_limit_bytes=FACE_LIMIT),
    )(field)


def side_columns(x0_ref, x1_ref, mix, side_ref):
    depth = x0_ref.shape[0]
    even, end = is_even("gx"), at_end("gx")
    mix[...] = jnp.zeros_like(mix)
    for k in range(depth):
        first, second = x0_ref[pl.ds(k, 1), :], drop(end, x1_ref[pl.ds(k, 1), :])
        mix[pl.ds(2 * k, 1), :] = pick(even, second, first)
        mix[pl.ds((2 * k + LANES - 1) % LANES, 1), :] = pick(even, first, second)
    side_ref[...] = mix[...].T


def rim_rows(f_ref, y0_ref, y1_ref, rim):
    depth, rows = f_ref.shape[1:3]
    even, end = is_even("gy"), at_end("gy")
    for half in range(2):
        for k in range(depth):
            first, second = y0_ref[half, pl.ds(k, 1), :], drop(end, y1_ref[half, pl.ds(k, 1), :])
            rim[0, half, k, pl.ds(7, 1), :] = pick(even, second, first)
            rim[0, half, k, pl.ds(8, 16), :] = f_ref[half, k, pl.ds(0, 16), :]
            rim[1, half, k, pl.ds(0, 16), :] = f_ref[half, k, pl.ds(rows - 16, 16), :]
            rim[1, half, k, pl.ds(16, 1), :] = pick(even, first, second)


def march_tile(density, depth, r, source, offset, side_ref, z0_ref, z1_ref):
    base = pl.multiple_of(r * 8, 8)
    lane = lax.broadcasted_iota(jnp.int32, (8, LANES), 1)
    is_first = lane == 0
    is_last = lane == LANES - 1
    ext_scale = 4.0 * density * LOG2E
    ext_base = 1.2 * density * LOG2E
    even, end = is_even("gz"), at_end("gz")

    def load(half, k, up):
        return source[half, k, pl.ds(offset + up, 8), :]

    def depth_halo(half, near):
        first = z0_ref[half, pl.ds(base, 8), :]
        second = drop(end, z1_ref[half, pl.ds(base, 8), :])
        return pick(even, second, first) if near else pick(even, first, second)

    packed = side_ref[pl.ds(base, 8), :]
    prev = [depth_halo(h, True) for h in range(2)]
    cur = [load(h, 0, 0) for h in range(2)]
    through = [jnp.ones((8, LANES), jnp.float32)] * 2
    total = [jnp.zeros((8, LANES), jnp.float32)] * 2
    tilted = [jnp.zeros((8, LANES), jnp.float32)] * 2
    bell = [jnp.zeros((8, LANES), jnp.float32)] * 2
    for k in range(depth):
        if k + 1 < depth:
            nxt = [load(h, k + 1, 0) for h in range(2)]
        else:
            nxt = [depth_halo(h, False) for h in range(2)]
        edge = pltpu.roll(packed, LANES - 2 * k, 1) if k else packed
        fwd = [pltpu.roll(c, LANES - 1, 1) for c in cur]
        bwd = [pltpu.roll(c, 1, 1) for c in cur]
        upper = [jnp.where(is_last, fwd[1], fwd[0]), jnp.where(is_last, edge, fwd[1])]
        lower = [jnp.where(is_first, edge, bwd[0]), jnp.where(is_first, bwd[0], bwd[1])]
        for h in range(2):
            f = cur[h]
            a = upper[h] - lower[h]
            b = load(h, k, 1) - load(h, k, -1)
            c = nxt[h] - prev[h]
            bc = b + c
            slope = jnp.abs((bc + bc) + a)
            inv = lax.rsqrt(((c * c + b * b) + 4.0) + a * a)
            t = jnp.tanh(f)
            gauss = jnp.exp2(f * (f * -LOG2E))
            keep = jnp.exp2((1.0 + t) * (inv * inv * ext_scale - ext_base))
            after = through[h] * keep
            w = through[h] - after
            ws = w * (1.0 + slope * inv)
            through[h] = after
            total[h] = total[h] + ws
            tilted[h] = tilted[h] + ws * t
            bell[h] = bell[h] + ws * gauss
        prev, cur = cur, nxt
    return [(total[h], tilted[h], bell[h], through[h]) for h in range(2)]


def first_kernel(density, f_ref, x0_ref, x1_ref, y0_ref, y1_ref, z0_ref, z1_ref, keep_ref, send_ref, side_ref, mix):
    depth = f_ref.shape[1]
    side_columns(x0_ref, x1_ref, mix, side_ref)
    even = is_even("gz")

    def step(band, carry):
        r = jnp.where(band == 0, 1, 2 * band)
        halves = march_tile(density, depth, r, f_ref, pl.multiple_of(r * 8, 8), side_ref, z0_ref, z1_ref)
        for c, (left, right) in enumerate(zip(*halves)):
            keep_ref[band, c] = pick(even, left, right)
            send_ref[band, c] = pick(even, right, left)
        return carry

    lax.fori_loop(0, BANDS, step, 0, unroll=4)


def rest_kernel(density, f_ref, side_ref, y0_ref, y1_ref, z0_ref, z1_ref, out_ref, rim):
    depth, rows = f_ref.shape[1:3]
    rim_rows(f_ref, y0_ref, y1_ref, rim)

    def tile(band, r, source, offset):
        halves = march_tile(density, depth, r, source, offset, side_ref, z0_ref, z1_ref)
        for half in range(2):
            for c in range(4):
                out_ref[band, half + 1, c] = halves[half][c]

    def step(band, carry):
        r = 2 * band + 1
        tile(band, r, f_ref, pl.multiple_of(r * 8, 8))
        return carry

    tile(0, jnp.int32(0), rim.at[0], 8)
    lax.fori_loop(1, BANDS - 1, step, 0, unroll=7)
    tile(BANDS - 1, jnp.int32(rows // 8 - 1), rim.at[1], 8)


def merge_kernel(own_ref, other_ref, parts_ref, out_ref):
    even = is_even("gz")

    def step(band, carry):
        mine = [own_ref[band, c] for c in range(4)]
        theirs = [other_ref[band, c] for c in range(4)]
        near = [pick(even, m, t) for m, t in zip(mine, theirs)]
        far = [pick(even, t, m) for m, t in zip(mine, theirs)]
        for c in range(3):
            out_ref[band, 0, c] = near[c] + near[3] * far[c]
        out_ref[band, 0, 3] = near[3] * far[3]
        return carry

    lax.fori_loop(0, BANDS, step, 0, unroll=4)


def call(kernel, shapes, scratch, args, cells=0, aliases={}):
    vmem = pl.BlockSpec(memory_space=pltpu.VMEM)
    cost = pl.CostEstimate(flops=40 * cells, bytes_accessed=4 * cells, transcendentals=4 * cells) if cells else None
    return pl.pallas_call(
        kernel,
        in_specs=[vmem] * len(args),
        out_specs=[vmem] * len(shapes),
        out_shape=[jax.ShapeDtypeStruct(shape, jnp.float32) for shape in shapes],
        scratch_shapes=scratch,
        input_output_aliases=aliases,
        cost_estimate=cost,
        compiler_params=pltpu.CompilerParams(vmem_limit_bytes=MARCH_LIMIT),
    )(*args)


def blend_kernel(parts_ref, out_ref):
    lone = lax.axis_index("gz") == 0
    for block, half, ids in (
        (0, 0, range(0, BANDS, 2)),
        (0, 1, range(1, BANDS, 2)),
        (1, 0, range(BANDS)),
        (2, 1, range(BANDS)),
    ):
        through = jnp.ones((8, LANES), jnp.float32)
        sums = [jnp.zeros((8, LANES), jnp.float32) for c in range(3)]
        for d in ids:
            for c in range(3):
                sums[c] = sums[c] + through * parts_ref[d, block, c]
            through = through * parts_ref[d, block, 3]
        where = jnp.where(lone, 8, 0) if block == 0 else jnp.where(lone, 0, 8)
        rows = pl.ds(pl.multiple_of(where, 8), 8)
        cols = pl.ds(half * LANES, LANES)
        out_ref[0, rows, cols] = (sums[0] + sums[1]) * 0.125
        out_ref[1, rows, cols] = sums[2] * 0.25
        out_ref[2, rows, cols] = (sums[0] - sums[1]) * 0.125
        out_ref[3, rows, cols] = 1.0 - through


def blend(parts, cols):
    return pl.pallas_call(
        blend_kernel,
        out_shape=jax.ShapeDtypeStruct((4, 16, cols), jnp.float32),
    )(parts)


def swap(block, axis, start):
    count = lax.axis_size(axis)
    pairs = []
    for i in range(start, count, 2):
        pairs += [(i, (i + 1) % count), ((i + 1) % count, i)]
    return lax.ppermute(block, axis, pairs)


def per_device(field):
    depth = field.shape[0]
    density = 4.0 / (depth * lax.axis_size("gz"))
    whole, x0, x1, y0, y1, z0, z1 = faces(field)
    z0, z1 = swap(z0, "gz", 0), swap(z1, "gz", 1)
    x0, x1 = swap(x0, "gx", 0), swap(x1, "gx", 1)
    y0, y1 = swap(y0, "gy", 0), swap(y1, "gy", 1)
    cells = depth * BANDS * 8 * field.shape[2]
    block = (BANDS, 4, 8, LANES)
    own, sent, side = call(
        functools.partial(first_kernel, density),
        [block, block, (BANDS * 16, LANES)],
        [pltpu.VMEM((LANES, BANDS * 16), jnp.float32)],
        (whole, x0, x1, y0, y1, z0, z1),
        cells,
    )
    other = swap(sent, "gz", 0)
    (parts,) = call(
        functools.partial(rest_kernel, density),
        [(BANDS, 3, 4, 8, LANES)],
        [pltpu.VMEM((2, 2, depth, 24, LANES), jnp.float32)],
        (whole, side, y0, y1, z0, z1),
        cells,
    )
    (parts,) = call(merge_kernel, [parts.shape], [], (own, other, parts), aliases={2: 0})
    parts = lax.all_to_all(parts, "gz", split_axis=0, concat_axis=0, tiled=True)
    return blend(parts, field.shape[2])


def solution(mesh):
    return jax.shard_map(
        per_device,
        mesh=mesh,
        in_specs=(P("gz", "gy", "gx"),),
        out_specs=P(None, ("gy", "gz"), "gx"),
        check_vma=False,
    )
```

time: 65.7 us -> 62.1 us (0.945)
  blocking collectives: 36.4 us -> 28.2 us
  starting transfers between devices: 9.2 us -> 14.2 us
    all_to_all x1, blocking collectives: 36.4 us -> 28.2 us  [per_device(): parts = lax.all_to_all(parts, 'gz', split_axis=0, concat_axis=0, tiled=True)]
    ppermute x6 -> x7, starting transfers between devices: 9.2 us -> 14.2 us  [swap(): return lax.ppermute(block, axis, pairs)]
    pallas_call x2 -> x4, Pallas kernels: 12.5 us -> 12.3 us  [the longest x3 10.5 us: call(): pl.pallas_call(kernel, in_specs=[vmem] * len(args), out_specs=[vmem] * le...]
    ppermute x6 -> x7, waiting for transfers between devices: 3.04 us -> 3.05 us  [swap(): return lax.ppermute(block, axis, pairs)]
  transfers between devices with their start and end apart: 6 -> 7, of which waited for: 2 -> 2; matrix products, arithmetic and copies ran while one was open for 0% -> 0% of each run, Pallas kernels for 0% -> 8%
where the time goes in v5:
time: 62.1 us; the launch traced here: 61.9 us
  blocking collectives  28.2 us (45%)
  Pallas kernels  16.5 us (27%)
  starting transfers between devices  14.2 us (23%)
  waiting for transfers between devices  3.05 us (5%)
    all_to_all x1, blocking collectives, per_device(): parts = lax.all_to_all(parts, 'gz', split_axis=0, concat_axis=0, tiled=True)  28.2 us
    ppermute x7, starting transfers between devices, swap(): return lax.ppermute(block, axis, pairs)  14.2 us
    pallas_call x3, Pallas kernels, call(): pl.pallas_call(kernel, in_specs=[vmem] * len(args), out_specs=[vmem] * le...  10.5 us
    pallas_call x1, Pallas kernels, faces(): pl.pallas_call(face_kernel, in_specs=[pl.BlockSpec(memory_space=pl.ANY)],...  4.17 us
    ppermute x7, waiting for transfers between devices, swap(): return lax.ppermute(block, axis, pairs)  3.05 us
    pallas_call x1, Pallas kernels, blend(): pl.pallas_call(blend_kernel, out_shape=jax.ShapeDtypeStruct((4, 16, cols)...  1.82 us
  transfers between devices with their start and end apart: 7, of which 2 were waited for; matrix products, arithmetic and copies ran while one was open for 0% of the time, Pallas kernels for 8%

profile of v5, /device:TPU:32, one launch (start us, length us, event | category | flops | bytes accessed | tf_op | source)
XLA Modules:
  0.0 61.9 jit_solution(1644456580759863068)
XLA Ops:
  0.0 4.2 %shard_map.17 = (f32[2,32,256,128]{3,2,1,0:T(8,128)S(1)}, f32[32,256]{1,0:T(8,128)S(1)}, f32[32,256]{1,0:T(8,128)S(1)}, f32[2,32,128]{2,1,0:T(8,128)S(1)}, f32[2...) custom-call(f32[32,256,256]{2,1,0:T(8,128)} %f_ref.1), custom_call_target="tpu_custom_call" | custom-call | tf_op jit(solution)/shard_map/pallas_call | solution.py:87
  4.2 1.9 %collective-permute-start.4 = (f32[2,256,128]{2,1,0:T(8,128)S(1)}, f32[2,256,128]{2,1,0:T(8,128)S(1)}, u32[]{:S(2)}, u32[]{:S(2)}) collective-permute-start(f32[2,256,128]{2,1,0:T(8,128)S(1)} %get-tuple-element.20), channel_id=1, source_target_pairs={{0,1},{1,0},{2,3},{3,2},{4,5},{5,4},{6,7},{7,6},{8,9},{9,8},{10,11... | collective-permute-start | bytes 786440 | tf_op jit(solution)/shard_map/ppermute | solution.py:278
  6.1 2.0 %collective-permute-start.5 = (f32[2,256,128]{2,1,0:T(8,128)S(1)}, f32[2,256,128]{2,1,0:T(8,128)S(1)}, u32[]{:S(2)}, u32[]{:S(2)}) collective-permute-start(f32[2,256,128]{2,1,0:T(8,128)S(1)} %get-tuple-element.21), channel_id=1, source_target_pairs={{1,2},{2,1},{3,4},{4,3},{5,6},{6,5},{7,8},{8,7},{9,10},{10,9},{11,... | collective-permute-start | bytes 786440 | tf_op jit(solution)/shard_map/ppermute | solution.py:278
  8.1 0.0 collective-permute-start
  8.1 1.7 %collective-permute-start.1 = (f32[32,256]{1,0:T(8,128)S(1)}, f32[32,256]{1,0:T(8,128)S(1)}, u32[]{:S(2)}, u32[]{:S(2)}) collective-permute-start(f32[32,256]{1,0:T(8,128)S(1)} %get-tuple-element.17), channel_id=1, source_target_pairs={{64,128},{128,64},{192,0},{0,192},{65,129},{129,65},{193,1},{1,193... | collective-permute-start | bytes 98312 | tf_op jit(solution)/shard_map/ppermute | solution.py:278
  9.8 1.5 %collective-permute-start.2 = (f32[2,32,128]{2,1,0:T(8,128)S(1)}, f32[2,32,128]{2,1,0:T(8,128)S(1)}, u32[]{:S(2)}, u32[]{:S(2)}) collective-permute-start(f32[2,32,128]{2,1,0:T(8,128)S(1)} %get-tuple-element.18), channel_id=1, source_target_pairs={{0,16},{16,0},{32,48},{48,32},{1,17},{17,1},{33,49},{49,33},{2,18}... | collective-permute-start | bytes 98312 | tf_op jit(solution)/shard_map/ppermute | solution.py:278
  11.3 0.0 collective-permute-done.x0_ref
  11.3 2.1 %collective-permute-start.3 = (f32[2,32,128]{2,1,0:T(8,128)S(1)}, f32[2,32,128]{2,1,0:T(8,128)S(1)}, u32[]{:S(2)}, u32[]{:S(2)}) collective-permute-start(f32[2,32,128]{2,1,0:T(8,128)S(1)} %get-tuple-element.19), channel_id=1, source_target_pairs={{16,32},{32,16},{48,0},{0,48},{17,33},{33,17},{49,1},{1,49},{18,34... | collective-permute-start | bytes 98312 | tf_op jit(solution)/shard_map/ppermute | solution.py:278
  13.4 0.0 collective-permute-done.1.x1_ref
  13.4 0.3 collective-permute-done.2.y0_ref
  13.7 2.7 %collective-permute-done.3.y1_ref = f32[2,32,128]{2,1,0:T(8,128)S(1)} collective-permute-done((f32[2,32,128]{2,1,0:T(8,128)S(1)}, f32[2,32,128]{2,1,0:T(8,128)S(1)}, u32[]{:S(2)}, u32[]{:S(2)}) %collective-permute-start.3) | collective-permute-done | bytes 32800 | tf_op jit(solution)/shard_map/ppermute | solution.py:278
  16.4 0.0 collective-permute-done.4.z0_ref
  16.4 0.0 collective-permute-done.5.z1_ref
  16.4 5.3 %shard_map.18 = (f32[16,4,8,128]{3,2,1,0:T(8,128)S(1)}, f32[16,4,8,128]{3,2,1,0:T(8,128)S(1)}, f32[256,128]{1,0:T(8,128)S(1)}) custom-call(f32[2,32,256,128]{3,2,1,0:T(8,128)S(1)} %get-tuple-element.15.f_ref, f32[32,256]{1,0:T(8,128)S(1)} %collective-permute-done.x0_ref, f32[32,256]{1,0:T(8,128)S(1)} %collective-permute-done.1.x1_ref, ...), custom_call_target="tpu_custom_call" | custom-call | flops 41943040 | bytes 4194304 | tf_op jit(solution)/shard_map/pallas_call | solution.py:231
  21.7 5.0 %collective-permute-start.6 = (f32[16,4,8,128]{3,2,1,0:T(8,128)S(1)}, f32[16,4,8,128]{3,2,1,0:T(8,128)S(1)}, u32[]{:S(2)}, u32[]{:S(2)}) collective-permute-start(f32[16,4,8,128]{3,2,1,0:T(8,128)S(1)} %get-tuple-element.23), channel_id=1, source_target_pairs={{0,1},{1,0},{2,3},{3,2},{4,5},{5,4},{6,7},{7,6},{8,9},{9,8},{10,11... | collective-permute-start | bytes 786440 | tf_op jit(solution)/shard_map/ppermute | solution.py:278
  26.7 5.2 %shard_map.19.parts_ref = f32[16,3,4,8,128]{4,3,2,1,0:T(8,128)S(1)} custom-call(f32[2,32,256,128]{3,2,1,0:T(8,128)S(1)} %get-tuple-element.15.f_ref, f32[256,128]{1,0:T(8,128)S(1)} %get-tuple-element.24.side_ref, f32[2,32,128]{2,1,0:T(8,128)S(1)} %collective-permute-done.2.y0_ref, f32[2,32,128]{2,1,0:T(8,128)S(1)} %collective-permute-done.3.y1_ref, ...), custom_call_target="tpu_custom_call" | custom-call | flops 41943040 | bytes 4194304 | tf_op jit(solution)/shard_map/pallas_call | solution.py:231
  31.8 0.0 collective-permute-done.6.other_ref
  31.9 0.1 shard_map.20
  31.9 28.2 %all_to_all.5.parts_ref = f32[16,3,4,8,128]{4,3,2,1,0:T(8,128)} all-to-all(f32[16,3,4,8,128]{4,3,2,1,0:T(8,128)S(1)} %shard_map.20), channel_id=1, replica_groups=mesh['gx'=4,'gy'=4,'gz'=16] {'gz'}, dimensions={0} | all-to-all | bytes 1572864 | tf_op jit(solution)/shard_map/all_to_all | solution.py:306
  60.1 1.8 %shard_map.21 = f32[4,16,256]{2,1,0:T(8,128)} custom-call(f32[16,3,4,8,128]{4,3,2,1,0:T(8,128)} %all_to_all.5.parts_ref), custom_call_target="tpu_custom_call" | custom-call | tf_op jit(solution)/shard_map/pallas_call | solution.py:267
Async XLA Ops:
  4.2 12.2 %collective-permute-start.4 = (f32[2,256,128]{2,1,0:T(8,128)S(1)}, f32[2,256,128]{2,1,0:T(8,128)S(1)}, u32[]{:S(2)}, u32[]{:S(2)}) collective-permute-start(f32[2,256,128]{2,1,0:T(8,128)S(1)} %get-tuple-element.20), channel_id=1, source_target_pairs={{0,1},{1,0},{2,3},{3,2},{4,5},{5,4},{6,7},{7,6},{8,9},{9,8},{10,11... | collective-permute-start | bytes 786440 | tf_op jit(solution)/shard_map/ppermute | solution.py:278
  6.1 10.3 %collective-permute-start.5 = (f32[2,256,128]{2,1,0:T(8,128)S(1)}, f32[2,256,128]{2,1,0:T(8,128)S(1)}, u32[]{:S(2)}, u32[]{:S(2)}) collective-permute-start(f32[2,256,128]{2,1,0:T(8,128)S(1)} %get-tuple-element.21), channel_id=1, source_target_pairs={{1,2},{2,1},{3,4},{4,3},{5,6},{6,5},{7,8},{8,7},{9,10},{10,9},{11,... | collective-permute-start | bytes 786440 | tf_op jit(solution)/shard_map/ppermute | solution.py:278
  8.1 3.2 %collective-permute-start = (f32[32,256]{1,0:T(8,128)S(1)}, f32[32,256]{1,0:T(8,128)S(1)}, u32[]{:S(2)}, u32[]{:S(2)}) collective-permute-start(f32[32,256]{1,0:T(8,128)S(1)} %get-tuple-element.16), channel_id=1, source_target_pairs={{0,64},{64,0},{128,192},{192,128},{1,65},{65,1},{129,193},{193,129... | collective-permute-start | bytes 98312 | tf_op jit(solution)/shard_map/ppermute | solution.py:278
  8.1 5.3 %collective-permute-start.1 = (f32[32,256]{1,0:T(8,128)S(1)}, f32[32,256]{1,0:T(8,128)S(1)}, u32[]{:S(2)}, u32[]{:S(2)}) collective-permute-start(f32[32,256]{1,0:T(8,128)S(1)} %get-tuple-element.17), channel_id=1, source_target_pairs={{64,128},{128,64},{192,0},{0,192},{65,129},{129,65},{193,1},{1,193... | collective-permute-start | bytes 98312 | tf_op jit(solution)/shard_map/ppermute | solution.py:278
  9.8 3.9 %collective-permute-start.2 = (f32[2,32,128]{2,1,0:T(8,128)S(1)}, f32[2,32,128]{2,1,0:T(8,128)S(1)}, u32[]{:S(2)}, u32[]{:S(2)}) collective-permute-start(f32[2,32,128]{2,1,0:T(8,128)S(1)} %get-tuple-element.18), channel_id=1, source_target_pairs={{0,16},{16,0},{32,48},{48,32},{1,17},{17,1},{33,49},{49,33},{2,18}... | collective-permute-start | bytes 98312 | tf_op jit(solution)/shard_map/ppermute | solution.py:278
  11.3 5.1 %collective-permute-start.3 = (f32[2,32,128]{2,1,0:T(8,128)S(1)}, f32[2,32,128]{2,1,0:T(8,128)S(1)}, u32[]{:S(2)}, u32[]{:S(2)}) collective-permute-start(f32[2,32,128]{2,1,0:T(8,128)S(1)} %get-tuple-element.19), channel_id=1, source_target_pairs={{16,32},{32,16},{48,0},{0,48},{17,33},{33,17},{49,1},{1,49},{18,34... | collective-permute-start | bytes 98312 | tf_op jit(solution)/shard_map/ppermute | solution.py:278
  21.7 10.2 %collective-permute-start.6 = (f32[16,4,8,128]{3,2,1,0:T(8,128)S(1)}, f32[16,4,8,128]{3,2,1,0:T(8,128)S(1)}, u32[]{:S(2)}, u32[]{:S(2)}) collective-permute-start(f32[16,4,8,128]{3,2,1,0:T(8,128)S(1)} %get-tuple-element.23), channel_id=1, source_target_pairs={{0,1},{1,0},{2,3},{3,2},{4,5},{5,4},{6,7},{7,6},{8,9},{9,8},{10,11... | collective-permute-start | bytes 786440 | tf_op jit(solution)/shard_map/ppermute | solution.py:278

commit v6 on v5

--- a/solution.py
+++ b/solution.py
@@ -32,7 +32,7 @@
     return jnp.where(jnp.broadcast_to(even, yes.shape), yes, no)
 
 
-def face_kernel(f_ref, out_ref, x0_ref, x1_ref, y0_ref, y1_ref, z0_ref, z1_ref, packed, sems):
+def face_kernel(f_ref, out_ref, x0_ref, x1_ref, y0_ref, y1_ref, packed, sems):
     depth, rows, cols = f_ref.shape
     part_rows = rows // PARTS
     lane = lax.broadcasted_iota(jnp.int32, (8, LANES), 1)
@@ -65,7 +65,7 @@
         return carry
 
     lax.fori_loop(0, PARTS, step, 0)
-    even_x, even_y, even_z = is_even("gx"), is_even("gy"), is_even("gz")
+    even_x, even_y = is_even("gx"), is_even("gy")
     turned = packed[...].T
     left, right = turned[0:depth], turned[depth : 2 * depth]
     x0_ref[...] = pick(even_x, right, left)
@@ -75,19 +75,16 @@
             low, high = out_ref[half, k, 0:1, :], out_ref[half, k, rows - 1 : rows, :]
             y0_ref[half, pl.ds(k, 1), :] = pick(even_y, high, low)
             y1_ref[half, pl.ds(k, 1), :] = pick(even_y, low, high)
-        near, far = out_ref[half, 0], out_ref[half, depth - 1]
-        z0_ref[half] = pick(even_z, far, near)
-        z1_ref[half] = pick(even_z, near, far)
 
 
 def faces(field):
     depth, rows, cols = field.shape
     vmem = pl.BlockSpec(memory_space=pltpu.VMEM)
-    shapes = [(2, depth, rows, LANES)] + [(depth, rows)] * 2 + [(2, depth, LANES)] * 2 + [(2, rows, LANES)] * 2
+    shapes = [(2, depth, rows, LANES)] + [(depth, rows)] * 2 + [(2, depth, LANES)] * 2
     return pl.pallas_call(
         face_kernel,
         in_specs=[pl.BlockSpec(memory_space=pl.ANY)],
-        out_specs=[vmem] * 7,
+        out_specs=[vmem] * 5,
         out_shape=[jax.ShapeDtypeStruct(shape, jnp.float32) for shape in shapes],
         scratch_shapes=[pltpu.VMEM((rows, LANES), jnp.float32), pltpu.SemaphoreType.DMA((2 * PARTS,))],
         compiler_params=pltpu.CompilerParams(vmem_limit_bytes=FACE_LIMIT),
@@ -130,8 +127,9 @@
         return source[half, k, pl.ds(offset + up, 8), :]
 
     def depth_halo(half, near):
-        first = z0_ref[half, pl.ds(base, 8), :]
-        second = drop(end, z1_ref[half, pl.ds(base, 8), :])
+        here = pl.ds(base, 8), pl.ds(half * LANES, LANES)
+        first = z0_ref[here]
+        second = drop(end, z1_ref[here])
         return pick(even, second, first) if near else pick(even, first, second)
 
     packed = side_ref[pl.ds(base, 8), :]
@@ -266,7 +264,10 @@
 def blend(parts, cols):
     return pl.pallas_call(
         blend_kernel,
+        in_specs=[pl.BlockSpec(memory_space=pltpu.VMEM)],
+        out_specs=pl.BlockSpec(memory_space=pltpu.VMEM),
         out_shape=jax.ShapeDtypeStruct((4, 16, cols), jnp.float32),
+        compiler_params=pltpu.CompilerParams(vmem_limit_bytes=MARCH_LIMIT),
     )(parts)
 
 
@@ -281,8 +282,10 @@
 def per_device(field):
     depth = field.shape[0]
     density = 4.0 / (depth * lax.axis_size("gz"))
-    whole, x0, x1, y0, y1, z0, z1 = faces(field)
-    z0, z1 = swap(z0, "gz", 0), swap(z1, "gz", 1)
+    even = is_even("gz")
+    z0 = swap(field[jnp.where(even, depth - 1, 0)], "gz", 0)
+    z1 = swap(field[jnp.where(even, 0, depth - 1)], "gz", 1)
+    whole, x0, x1, y0, y1 = faces(field)
     x0, x1 = swap(x0, "gx", 0), swap(x1, "gx", 1)
     y0, y1 = swap(y0, "gy", 0), swap(y1, "gy", 1)
     cells = depth * BANDS * 8 * field.shape[2]

time: 62.1 us -> 60.6 us (0.976)
  blocking collectives: 28.2 us -> 26.7 us
  Pallas kernels: 16.5 us -> 15.4 us
  local copies, waits for them, and re-layouts: 0 us -> 1.06 us
    all_to_all x1, blocking collectives: 28.2 us -> 26.7 us  [per_device(): parts = lax.all_to_all(parts, 'gz', split_axis=0, concat_axis=0, tiled=True)]
    pallas_call x1, Pallas kernels: 1.82 us -> 0.68 us  [blend(): pl.pallas_call(blend_kernel, in_specs=[pl.BlockSpec(memory_space=pltpu.VM...]
    squeeze x0 -> x1, local copies, waits for them, and re-layouts: none -> 1.06 us  [per_device(): z1 = swap(field[jnp.where(even, 0, depth - 1)], 'gz', 1)]
  transfers between devices with their start and end apart: 7 -> 7, of which waited for: 2 -> 2; matrix products, arithmetic and copies ran while one was open for 0% -> 0% of each run, Pallas kernels for 8% -> 15%
where the time goes in v6:
time: 60.6 us; the launch traced here: 60.5 us
  blocking collectives  26.7 us (44%)
  Pallas kernels  15.4 us (25%)
  starting transfers between devices  14.3 us (24%)
  waiting for transfers between devices  3.04 us (5%)
  local copies, waits for them, and re-layouts  1.06 us (2%)
    all_to_all x1, blocking collectives, per_device(): parts = lax.all_to_all(parts, 'gz', split_axis=0, concat_axis=0, tiled=True)  26.7 us
    ppermute x7, starting transfers between devices, swap(): return lax.ppermute(block, axis, pairs)  14.3 us
    pallas_call x3, Pallas kernels, call(): pl.pallas_call(kernel, in_specs=[vmem] * len(args), out_specs=[vmem] * le...  10.6 us
    pallas_call x1, Pallas kernels, faces(): pl.pallas_call(face_kernel, in_specs=[pl.BlockSpec(memory_space=pl.ANY)],...  4.15 us
    ppermute x7, waiting for transfers between devices, swap(): return lax.ppermute(block, axis, pairs)  3.04 us
  transfers between devices with their start and end apart: 7, of which 2 were waited for; matrix products, arithmetic and copies ran while one was open for 0% of the time, Pallas kernels for 15%

profile of v6, /device:TPU:32, one launch (start us, length us, event | category | flops | bytes accessed | tf_op | source)
XLA Modules:
  0.0 60.5 jit_solution(17555460049405676663)
XLA Ops:
  0.0 1.1 %dynamic-slice_bitcast_fusion = (f32[256,256]{1,0:T(8,128)S(1)}, f32[256,256]{1,0:T(8,128)S(1)}) fusion(f32[32,256,256]{2,1,0:T(8,128)} %f_ref.1, s32[]{:T(128)S(6)} %select_n.10, s32[]{:T(128)S(6)} %select_n.9), kind=kLoop, calls=%fused_computation | loop fusion | bytes 1048584 | tf_op jit(solution)/shard_map/squeeze | solution.py:287
  1.1 1.9 %collective-permute-start.4 = (f32[256,256]{1,0:T(8,128)S(1)}, f32[256,256]{1,0:T(8,128)S(1)}, u32[]{:S(2)}, u32[]{:S(2)}) collective-permute-start(f32[256,256]{1,0:T(8,128)S(1)} %get-tuple-element.22), channel_id=1, source_target_pairs={{0,1},{1,0},{2,3},{3,2},{4,5},{5,4},{6,7},{7,6},{8,9},{9,8},{10,11... | collective-permute-start | bytes 786440 | tf_op jit(solution)/shard_map/ppermute | solution.py:279
  3.0 2.0 %collective-permute-start.5 = (f32[256,256]{1,0:T(8,128)S(1)}, f32[256,256]{1,0:T(8,128)S(1)}, u32[]{:S(2)}, u32[]{:S(2)}) collective-permute-start(f32[256,256]{1,0:T(8,128)S(1)} %get-tuple-element.21), channel_id=1, source_target_pairs={{1,2},{2,1},{3,4},{4,3},{5,6},{6,5},{7,8},{8,7},{9,10},{10,9},{11,... | collective-permute-start | bytes 786440 | tf_op jit(solution)/shard_map/ppermute | solution.py:279
  5.0 4.2 %shard_map.17 = (f32[2,32,256,128]{3,2,1,0:T(8,128)S(1)}, f32[32,256]{1,0:T(8,128)S(1)}, f32[32,256]{1,0:T(8,128)S(1)}, f32[2,32,128]{2,1,0:T(8,128)S(1)}, f32[2,32,128]{2,1,0:T(8,128)S(1)}) custom-call(f32[32,256,256]{2,1,0:T(8,128)} %f_ref.1), custom_call_target="tpu_custom_call" | custom-call | tf_op jit(solution)/shard_map/pallas_call | solution.py:84
  9.1 0.1 collective-permute-start
  9.2 1.7 %collective-permute-start.1 = (f32[32,256]{1,0:T(8,128)S(1)}, f32[32,256]{1,0:T(8,128)S(1)}, u32[]{:S(2)}, u32[]{:S(2)}) collective-permute-start(f32[32,256]{1,0:T(8,128)S(1)} %get-tuple-element.15), channel_id=1, source_target_pairs={{64,128},{128,64},{192,0},{0,192},{65,129},{129,65},{193,1},{1,193... | collective-permute-start | bytes 98312 | tf_op jit(solution)/shard_map/ppermute | solution.py:279
  10.9 1.5 %collective-permute-start.2 = (f32[2,32,128]{2,1,0:T(8,128)S(1)}, f32[2,32,128]{2,1,0:T(8,128)S(1)}, u32[]{:S(2)}, u32[]{:S(2)}) collective-permute-start(f32[2,32,128]{2,1,0:T(8,128)S(1)} %get-tuple-element.16), channel_id=1, source_target_pairs={{0,16},{16,0},{32,48},{48,32},{1,17},{17,1},{33,49},{49,33},{2,18}... | collective-permute-start | bytes 98312 | tf_op jit(solution)/shard_map/ppermute | solution.py:279
  12.4 0.0 collective-permute-done.x0_ref
  12.4 2.1 %collective-permute-start.3 = (f32[2,32,128]{2,1,0:T(8,128)S(1)}, f32[2,32,128]{2,1,0:T(8,128)S(1)}, u32[]{:S(2)}, u32[]{:S(2)}) collective-permute-start(f32[2,32,128]{2,1,0:T(8,128)S(1)} %get-tuple-element.17), channel_id=1, source_target_pairs={{16,32},{32,16},{48,0},{0,48},{17,33},{33,17},{49,1},{1,49},{18,34... | collective-permute-start | bytes 98312 | tf_op jit(solution)/shard_map/ppermute | solution.py:279
  14.5 0.0 collective-permute-done.1.x1_ref
  14.5 0.3 collective-permute-done.2.y0_ref
  14.9 2.7 %collective-permute-done.3.y1_ref = f32[2,32,128]{2,1,0:T(8,128)S(1)} collective-permute-done((f32[2,32,128]{2,1,0:T(8,128)S(1)}, f32[2,32,128]{2,1,0:T(8,128)S(1)}, u32[]{:S(2)}, u32[]{:S(2)}) %collective-permute-start.3) | collective-permute-done | bytes 32800 | tf_op jit(solution)/shard_map/ppermute | solution.py:279
  17.6 0.0 collective-permute-done.4.z0_ref
  17.6 0.0 collective-permute-done.5.z1_ref
  17.6 5.3 %shard_map.18 = (f32[16,4,8,128]{3,2,1,0:T(8,128)S(1)}, f32[16,4,8,128]{3,2,1,0:T(8,128)S(1)}, f32[256,128]{1,0:T(8,128)S(1)}) custom-call(f32[2,32,256,128]{3,2,1,0:T(8,128)S(1)} %get-tuple-element.13.f_ref, f32[32,256]{1,0:T(8,128)S(1)} %collective-permute-done.x0_ref, f32[32,256]{1,0:T(8,128)S(1)} %collective-permute-done.1.x1_ref, ...), custom_call_target="tpu_custom_call" | custom-call | flops 41943040 | bytes 4194304 | tf_op jit(solution)/shard_map/pallas_call | solution.py:229
  22.9 5.0 %collective-permute-start.6 = (f32[16,4,8,128]{3,2,1,0:T(8,128)S(1)}, f32[16,4,8,128]{3,2,1,0:T(8,128)S(1)}, u32[]{:S(2)}, u32[]{:S(2)}) collective-permute-start(f32[16,4,8,128]{3,2,1,0:T(8,128)S(1)} %get-tuple-element.19), channel_id=1, source_target_pairs={{0,1},{1,0},{2,3},{3,2},{4,5},{5,4},{6,7},{7,6},{8,9},{9,8},{10,11... | collective-permute-start | bytes 786440 | tf_op jit(solution)/shard_map/ppermute | solution.py:279
  27.8 5.2 %shard_map.19.parts_ref = f32[16,3,4,8,128]{4,3,2,1,0:T(8,128)S(1)} custom-call(f32[2,32,256,128]{3,2,1,0:T(8,128)S(1)} %get-tuple-element.13.f_ref, f32[256,128]{1,0:T(8,128)S(1)} %get-tuple-element.20.side_ref, f32[2,32,128]{2,1,0:T(8,128)S(1)} %collective-permute-done.2.y0_ref, f32[2,32,128]{2,1,0:T(8,128)S(1)} %collective-permute-done.3.y1_ref, ...), custom_call_target="tpu_custom_call" | custom-call | flops 41943040 | bytes 4194304 | tf_op jit(solution)/shard_map/pallas_call | solution.py:229
  33.0 0.0 collective-permute-done.6.other_ref
  33.0 0.1 shard_map.20
  33.1 26.7 %all_to_all.5.parts_ref = f32[16,3,4,8,128]{4,3,2,1,0:T(8,128)S(1)} all-to-all(f32[16,3,4,8,128]{4,3,2,1,0:T(8,128)S(1)} %shard_map.20), channel_id=1, replica_groups=mesh['gx'=4,'gy'=4,'gz'=16] {'gz'}, dimensions={0} | all-to-all | bytes 1572864 | tf_op jit(solution)/shard_map/all_to_all | solution.py:309
  59.8 0.7 %shard_map.21 = f32[4,16,256]{2,1,0:T(8,128)} custom-call(f32[16,3,4,8,128]{4,3,2,1,0:T(8,128)S(1)} %all_to_all.5.parts_ref), custom_call_target="tpu_custom_call" | custom-call | tf_op jit(solution)/shard_map/pallas_call | solution.py:265
Async XLA Ops:
  1.1 16.5 %collective-permute-start.4 = (f32[256,256]{1,0:T(8,128)S(1)}, f32[256,256]{1,0:T(8,128)S(1)}, u32[]{:S(2)}, u32[]{:S(2)}) collective-permute-start(f32[256,256]{1,0:T(8,128)S(1)} %get-tuple-element.22), channel_id=1, source_target_pairs={{0,1},{1,0},{2,3},{3,2},{4,5},{5,4},{6,7},{7,6},{8,9},{9,8},{10,11... | collective-permute-start | bytes 786440 | tf_op jit(solution)/shard_map/ppermute | solution.py:279
  3.0 14.6 %collective-permute-start.5 = (f32[256,256]{1,0:T(8,128)S(1)}, f32[256,256]{1,0:T(8,128)S(1)}, u32[]{:S(2)}, u32[]{:S(2)}) collective-permute-start(f32[256,256]{1,0:T(8,128)S(1)} %get-tuple-element.21), channel_id=1, source_target_pairs={{1,2},{2,1},{3,4},{4,3},{5,6},{6,5},{7,8},{8,7},{9,10},{10,9},{11,... | collective-permute-start | bytes 786440 | tf_op jit(solution)/shard_map/ppermute | solution.py:279
  9.1 3.3 %collective-permute-start = (f32[32,256]{1,0:T(8,128)S(1)}, f32[32,256]{1,0:T(8,128)S(1)}, u32[]{:S(2)}, u32[]{:S(2)}) collective-permute-start(f32[32,256]{1,0:T(8,128)S(1)} %get-tuple-element.14), channel_id=1, source_target_pairs={{0,64},{64,0},{128,192},{192,128},{1,65},{65,1},{129,193},{193,129... | collective-permute-start | bytes 98312 | tf_op jit(solution)/shard_map/ppermute | solution.py:279
  9.2 5.3 %collective-permute-start.1 = (f32[32,256]{1,0:T(8,128)S(1)}, f32[32,256]{1,0:T(8,128)S(1)}, u32[]{:S(2)}, u32[]{:S(2)}) collective-permute-start(f32[32,256]{1,0:T(8,128)S(1)} %get-tuple-element.15), channel_id=1, source_target_pairs={{64,128},{128,64},{192,0},{0,192},{65,129},{129,65},{193,1},{1,193... | collective-permute-start | bytes 98312 | tf_op jit(solution)/shard_map/ppermute | solution.py:279
  10.9 3.9 %collective-permute-start.2 = (f32[2,32,128]{2,1,0:T(8,128)S(1)}, f32[2,32,128]{2,1,0:T(8,128)S(1)}, u32[]{:S(2)}, u32[]{:S(2)}) collective-permute-start(f32[2,32,128]{2,1,0:T(8,128)S(1)} %get-tuple-element.16), channel_id=1, source_target_pairs={{0,16},{16,0},{32,48},{48,32},{1,17},{17,1},{33,49},{49,33},{2,18}... | collective-permute-start | bytes 98312 | tf_op jit(solution)/shard_map/ppermute | solution.py:279
  12.4 5.1 %collective-permute-start.3 = (f32[2,32,128]{2,1,0:T(8,128)S(1)}, f32[2,32,128]{2,1,0:T(8,128)S(1)}, u32[]{:S(2)}, u32[]{:S(2)}) collective-permute-start(f32[2,32,128]{2,1,0:T(8,128)S(1)} %get-tuple-element.17), channel_id=1, source_target_pairs={{16,32},{32,16},{48,0},{0,48},{17,33},{33,17},{49,1},{1,49},{18,34... | collective-permute-start | bytes 98312 | tf_op jit(solution)/shard_map/ppermute | solution.py:279
  22.9 10.1 %collective-permute-start.6 = (f32[16,4,8,128]{3,2,1,0:T(8,128)S(1)}, f32[16,4,8,128]{3,2,1,0:T(8,128)S(1)}, u32[]{:S(2)}, u32[]{:S(2)}) collective-permute-start(f32[16,4,8,128]{3,2,1,0:T(8,128)S(1)} %get-tuple-element.19), channel_id=1, source_target_pairs={{0,1},{1,0},{2,3},{3,2},{4,5},{5,4},{6,7},{7,6},{8,9},{9,8},{10,11... | collective-permute-start | bytes 786440 | tf_op jit(solution)/shard_map/ppermute | solution.py:279

commit v7 on v6

--- a/solution.py
+++ b/solution.py
@@ -184,7 +184,7 @@
             send_ref[band, c] = pick(even, right, left)
         return carry
 
-    lax.fori_loop(0, BANDS, step, 0, unroll=4)
+    lax.fori_loop(0, BANDS, step, 0, unroll=8)
 
 
 def rest_kernel(density, f_ref, side_ref, y0_ref, y1_ref, z0_ref, z1_ref, out_ref, rim):

time: 60.6 us -> 60.5 us (level)
  no operation moved by 1% of the time
where the time goes in v7:
time: 60.5 us; the launch traced here: 60.4 us
  blocking collectives  26.7 us (44%)
  Pallas kernels  15.3 us (25%)
  starting transfers between devices  14.3 us (24%)
  waiting for transfers between devices  3.04 us (5%)
  local copies, waits for them, and re-layouts  1.06 us (2%)
    all_to_all x1, blocking collectives, per_device(): parts = lax.all_to_all(parts, 'gz', split_axis=0, concat_axis=0, tiled=True)  26.7 us
    ppermute x7, starting transfers between devices, swap(): return lax.ppermute(block, axis, pairs)  14.3 us
    pallas_call x3, Pallas kernels, call(): pl.pallas_call(kernel, in_specs=[vmem] * len(args), out_specs=[vmem] * le...  10.5 us
    pallas_call x1, Pallas kernels, faces(): pl.pallas_call(face_kernel, in_specs=[pl.BlockSpec(memory_space=pl.ANY)],...  4.15 us
    ppermute x7, waiting for transfers between devices, swap(): return lax.ppermute(block, axis, pairs)  3.04 us
  transfers between devices with their start and end apart: 7, of which 2 were waited for; matrix products, arithmetic and copies ran while one was open for 0% of the time, Pallas kernels for 15%

profile of v7, /device:TPU:32, one launch (start us, length us, event | category | flops | bytes accessed | tf_op | source)
XLA Modules:
  0.0 60.4 jit_solution(518535934246720437)
XLA Ops:
  0.0 1.1 %dynamic-slice_bitcast_fusion = (f32[256,256]{1,0:T(8,128)S(1)}, f32[256,256]{1,0:T(8,128)S(1)}) fusion(f32[32,256,256]{2,1,0:T(8,128)} %f_ref.1, s32[]{:T(128)S(6)} %select_n.10, s32[]{:T(128)S(6)} %select_n.9), kind=kLoop, calls=%fused_computation | loop fusion | bytes 1048584 | tf_op jit(solution)/shard_map/squeeze | solution.py:287
  1.1 1.9 %collective-permute-start.4 = (f32[256,256]{1,0:T(8,128)S(1)}, f32[256,256]{1,0:T(8,128)S(1)}, u32[]{:S(2)}, u32[]{:S(2)}) collective-permute-start(f32[256,256]{1,0:T(8,128)S(1)} %get-tuple-element.22), channel_id=1, source_target_pairs={{0,1},{1,0},{2,3},{3,2},{4,5},{5,4},{6,7},{7,6},{8,9},{9,8},{10,11... | collective-permute-start | bytes 786440 | tf_op jit(solution)/shard_map/ppermute | solution.py:279
  3.0 2.0 %collective-permute-start.5 = (f32[256,256]{1,0:T(8,128)S(1)}, f32[256,256]{1,0:T(8,128)S(1)}, u32[]{:S(2)}, u32[]{:S(2)}) collective-permute-start(f32[256,256]{1,0:T(8,128)S(1)} %get-tuple-element.21), channel_id=1, source_target_pairs={{1,2},{2,1},{3,4},{4,3},{5,6},{6,5},{7,8},{8,7},{9,10},{10,9},{11,... | collective-permute-start | bytes 786440 | tf_op jit(solution)/shard_map/ppermute | solution.py:279
  5.0 4.2 %shard_map.17 = (f32[2,32,256,128]{3,2,1,0:T(8,128)S(1)}, f32[32,256]{1,0:T(8,128)S(1)}, f32[32,256]{1,0:T(8,128)S(1)}, f32[2,32,128]{2,1,0:T(8,128)S(1)}, f32[2,32,128]{2,1,0:T(8,128)S(1)}) custom-call(f32[32,256,256]{2,1,0:T(8,128)} %f_ref.1), custom_call_target="tpu_custom_call" | custom-call | tf_op jit(solution)/shard_map/pallas_call | solution.py:84
  9.1 0.1 collective-permute-start
  9.2 1.7 %collective-permute-start.1 = (f32[32,256]{1,0:T(8,128)S(1)}, f32[32,256]{1,0:T(8,128)S(1)}, u32[]{:S(2)}, u32[]{:S(2)}) collective-permute-start(f32[32,256]{1,0:T(8,128)S(1)} %get-tuple-element.15), channel_id=1, source_target_pairs={{64,128},{128,64},{192,0},{0,192},{65,129},{129,65},{193,1},{1,193... | collective-permute-start | bytes 98312 | tf_op jit(solution)/shard_map/ppermute | solution.py:279
  10.9 1.5 %collective-permute-start.2 = (f32[2,32,128]{2,1,0:T(8,128)S(1)}, f32[2,32,128]{2,1,0:T(8,128)S(1)}, u32[]{:S(2)}, u32[]{:S(2)}) collective-permute-start(f32[2,32,128]{2,1,0:T(8,128)S(1)} %get-tuple-element.16), channel_id=1, source_target_pairs={{0,16},{16,0},{32,48},{48,32},{1,17},{17,1},{33,49},{49,33},{2,18}... | collective-permute-start | bytes 98312 | tf_op jit(solution)/shard_map/ppermute | solution.py:279
  12.4 0.0 collective-permute-done.x0_ref
  12.4 2.1 %collective-permute-start.3 = (f32[2,32,128]{2,1,0:T(8,128)S(1)}, f32[2,32,128]{2,1,0:T(8,128)S(1)}, u32[]{:S(2)}, u32[]{:S(2)}) collective-permute-start(f32[2,32,128]{2,1,0:T(8,128)S(1)} %get-tuple-element.17), channel_id=1, source_target_pairs={{16,32},{32,16},{48,0},{0,48},{17,33},{33,17},{49,1},{1,49},{18,34... | collective-permute-start | bytes 98312 | tf_op jit(solution)/shard_map/ppermute | solution.py:279
  14.5 0.0 collective-permute-done.1.x1_ref
  14.5 0.3 collective-permute-done.2.y0_ref
  14.9 2.7 %collective-permute-done.3.y1_ref = f32[2,32,128]{2,1,0:T(8,128)S(1)} collective-permute-done((f32[2,32,128]{2,1,0:T(8,128)S(1)}, f32[2,32,128]{2,1,0:T(8,128)S(1)}, u32[]{:S(2)}, u32[]{:S(2)}) %collective-permute-start.3) | collective-permute-done | bytes 32800 | tf_op jit(solution)/shard_map/ppermute | solution.py:279
  17.6 0.0 collective-permute-done.4.z0_ref
  17.6 0.0 collective-permute-done.5.z1_ref
  17.6 5.2 %shard_map.18 = (f32[16,4,8,128]{3,2,1,0:T(8,128)S(1)}, f32[16,4,8,128]{3,2,1,0:T(8,128)S(1)}, f32[256,128]{1,0:T(8,128)S(1)}) custom-call(f32[2,32,256,128]{3,2,1,0:T(8,128)S(1)} %get-tuple-element.13.f_ref, f32[32,256]{1,0:T(8,128)S(1)} %collective-permute-done.x0_ref, f32[32,256]{1,0:T(8,128)S(1)} %collective-permute-done.1.x1_ref, ...), custom_call_target="tpu_custom_call" | custom-call | flops 41943040 | bytes 4194304 | tf_op jit(solution)/shard_map/pallas_call | solution.py:229
  22.8 5.0 %collective-permute-start.6 = (f32[16,4,8,128]{3,2,1,0:T(8,128)S(1)}, f32[16,4,8,128]{3,2,1,0:T(8,128)S(1)}, u32[]{:S(2)}, u32[]{:S(2)}) collective-permute-start(f32[16,4,8,128]{3,2,1,0:T(8,128)S(1)} %get-tuple-element.19), channel_id=1, source_target_pairs={{0,1},{1,0},{2,3},{3,2},{4,5},{5,4},{6,7},{7,6},{8,9},{9,8},{10,11... | collective-permute-start | bytes 786440 | tf_op jit(solution)/shard_map/ppermute | solution.py:279
  27.7 5.2 %shard_map.19.parts_ref = f32[16,3,4,8,128]{4,3,2,1,0:T(8,128)S(1)} custom-call(f32[2,32,256,128]{3,2,1,0:T(8,128)S(1)} %get-tuple-element.13.f_ref, f32[256,128]{1,0:T(8,128)S(1)} %get-tuple-element.20.side_ref, f32[2,32,128]{2,1,0:T(8,128)S(1)} %collective-permute-done.2.y0_ref, f32[2,32,128]{2,1,0:T(8,128)S(1)} %collective-permute-done.3.y1_ref, ...), custom_call_target="tpu_custom_call" | custom-call | flops 41943040 | bytes 4194304 | tf_op jit(solution)/shard_map/pallas_call | solution.py:229
  32.9 0.0 collective-permute-done.6.other_ref
  32.9 0.1 shard_map.20
  33.0 26.7 %all_to_all.5.parts_ref = f32[16,3,4,8,128]{4,3,2,1,0:T(8,128)S(1)} all-to-all(f32[16,3,4,8,128]{4,3,2,1,0:T(8,128)S(1)} %shard_map.20), channel_id=1, replica_groups=mesh['gx'=4,'gy'=4,'gz'=16] {'gz'}, dimensions={0} | all-to-all | bytes 1572864 | tf_op jit(solution)/shard_map/all_to_all | solution.py:309
  59.7 0.7 %shard_map.21 = f32[4,16,256]{2,1,0:T(8,128)} custom-call(f32[16,3,4,8,128]{4,3,2,1,0:T(8,128)S(1)} %all_to_all.5.parts_ref), custom_call_target="tpu_custom_call" | custom-call | tf_op jit(solution)/shard_map/pallas_call | solution.py:265
Async XLA Ops:
  1.1 16.5 %collective-permute-start.4 = (f32[256,256]{1,0:T(8,128)S(1)}, f32[256,256]{1,0:T(8,128)S(1)}, u32[]{:S(2)}, u32[]{:S(2)}) collective-permute-start(f32[256,256]{1,0:T(8,128)S(1)} %get-tuple-element.22), channel_id=1, source_target_pairs={{0,1},{1,0},{2,3},{3,2},{4,5},{5,4},{6,7},{7,6},{8,9},{9,8},{10,11... | collective-permute-start | bytes 786440 | tf_op jit(solution)/shard_map/ppermute | solution.py:279
  3.0 14.6 %collective-permute-start.5 = (f32[256,256]{1,0:T(8,128)S(1)}, f32[256,256]{1,0:T(8,128)S(1)}, u32[]{:S(2)}, u32[]{:S(2)}) collective-permute-start(f32[256,256]{1,0:T(8,128)S(1)} %get-tuple-element.21), channel_id=1, source_target_pairs={{1,2},{2,1},{3,4},{4,3},{5,6},{6,5},{7,8},{8,7},{9,10},{10,9},{11,... | collective-permute-start | bytes 786440 | tf_op jit(solution)/shard_map/ppermute | solution.py:279
  9.1 3.3 %collective-permute-start = (f32[32,256]{1,0:T(8,128)S(1)}, f32[32,256]{1,0:T(8,128)S(1)}, u32[]{:S(2)}, u32[]{:S(2)}) collective-permute-start(f32[32,256]{1,0:T(8,128)S(1)} %get-tuple-element.14), channel_id=1, source_target_pairs={{0,64},{64,0},{128,192},{192,128},{1,65},{65,1},{129,193},{193,129... | collective-permute-start | bytes 98312 | tf_op jit(solution)/shard_map/ppermute | solution.py:279
  9.2 5.3 %collective-permute-start.1 = (f32[32,256]{1,0:T(8,128)S(1)}, f32[32,256]{1,0:T(8,128)S(1)}, u32[]{:S(2)}, u32[]{:S(2)}) collective-permute-start(f32[32,256]{1,0:T(8,128)S(1)} %get-tuple-element.15), channel_id=1, source_target_pairs={{64,128},{128,64},{192,0},{0,192},{65,129},{129,65},{193,1},{1,193... | collective-permute-start | bytes 98312 | tf_op jit(solution)/shard_map/ppermute | solution.py:279
  10.9 3.9 %collective-permute-start.2 = (f32[2,32,128]{2,1,0:T(8,128)S(1)}, f32[2,32,128]{2,1,0:T(8,128)S(1)}, u32[]{:S(2)}, u32[]{:S(2)}) collective-permute-start(f32[2,32,128]{2,1,0:T(8,128)S(1)} %get-tuple-element.16), channel_id=1, source_target_pairs={{0,16},{16,0},{32,48},{48,32},{1,17},{17,1},{33,49},{49,33},{2,18}... | collective-permute-start | bytes 98312 | tf_op jit(solution)/shard_map/ppermute | solution.py:279
  12.4 5.1 %collective-permute-start.3 = (f32[2,32,128]{2,1,0:T(8,128)S(1)}, f32[2,32,128]{2,1,0:T(8,128)S(1)}, u32[]{:S(2)}, u32[]{:S(2)}) collective-permute-start(f32[2,32,128]{2,1,0:T(8,128)S(1)} %get-tuple-element.17), channel_id=1, source_target_pairs={{16,32},{32,16},{48,0},{0,48},{17,33},{33,17},{49,1},{1,49},{18,34... | collective-permute-start | bytes 98312 | tf_op jit(solution)/shard_map/ppermute | solution.py:279
  22.8 10.1 %collective-permute-start.6 = (f32[16,4,8,128]{3,2,1,0:T(8,128)S(1)}, f32[16,4,8,128]{3,2,1,0:T(8,128)S(1)}, u32[]{:S(2)}, u32[]{:S(2)}) collective-permute-start(f32[16,4,8,128]{3,2,1,0:T(8,128)S(1)} %get-tuple-element.19), channel_id=1, source_target_pairs={{0,1},{1,0},{2,3},{3,2},{4,5},{5,4},{6,7},{7,6},{8,9},{9,8},{10,11... | collective-permute-start | bytes 786440 | tf_op jit(solution)/shard_map/ppermute | solution.py:279
